TPU v7x, 512 devices: a whole 4x4x16 slice. The times are simulated.
512 devices in a mesh: row: 16 (over x, z_lo), col: 32 (over y, z_hi, core).
Axes of the slice: x: 4, y: 4, z: 16 (z_hi: 4, z_lo: 4; z = z_hi * 4 + z_lo), core: 2. Of those that a mesh axis runs over, the one named last changes fastest.
Arguments:
- queries: bfloat16 [16, 32, 128, 512], P(None, 'col', 'row'), may hold values from -6 to 6
- grad_output: bfloat16 [16, 32, 128, 512], P(None, 'col', 'row'), may hold values from -60 to 60
- attn_output: bfloat16 [16, 32, 128, 512], P(None, 'col', 'row'), may hold values from -1.796875 to 1.796875
- key_states: bfloat16 [65536, 128], P(('row', 'col')), may hold values from -6 to 6
- value_states: bfloat16 [65536, 128], P(('row', 'col')), may hold values from -6 to 6
- log_sum: float32 [16, 32, 128, 4], P(None, 'col', 'row'), may hold values from -1 to 12
- segment: int32 [65536], replicated, may hold values from 0 to 10, as said below
- prefix: int32 [65536], replicated, may hold values from 0 to 10, as said below
- block_list: int32 [16, 32, 16, 32], P(None, 'col', 'row'), may hold values from 0 to 31, as said below
- block_count: int32 [16, 32, 16], P(None, 'col', 'row'), may hold values from 0 to 32
Outputs:
- grad_query: bfloat16 [16, 32, 128, 512], P(None, 'col', 'row')
- grad_key: bfloat16 [65536, 128], P(('row', 'col'))
- grad_value: bfloat16 [65536, 128], P(('row', 'col'))
Inputs may be any that keep to these rules, and one draw needn't show every extreme that they name: Non-decreasing along the pack, each segment a nonempty run of positions; segment 0 is a prompt that covers the first 8192 positions and segment 1 is a response to it. `prefix`: segment[p] itself for a position of a prompt; for a position of a response, the id of an earlier prompt segment, the same for the whole response. `block_list`: for query block (j, c) and key group g, the key blocks of the group (numbered within it) that hold a key allowed to some query of the block by the segment and causal rules, ascending in the first block_count[j, c, g] entries; the other entries are 0.
All inputs are finite; a program needn't handle non-finite values.
Results may differ from a plain program's by a relative error of at most 0.015.
Values may be sent and summed in bfloat16 or wider, within the bound.
No kernel may reach another device: no remote copies, remote signals or barrier semaphores. Data moves between devices by JAX's collectives and lax.ppermute only.
A program may use at most 64 MiB of HBM per device.

v0:
```python
import functools

import jax
import jax.numpy as jnp
from jax import lax
from jax.experimental import pallas as pl
from jax.experimental.pallas import tpu as pltpu
from jax.sharding import PartitionSpec as P

NX, NZL, NY, NZH, NCORE = 4, 4, 4, 4, 2
SEGMENTS = 11
LOG2E = 1.4426950408889634
NEVER = -(1 << 30)


def row_perm(dx, dzl):
    return [
        (x * NZL + z, ((x + dx) % NX) * NZL + (z + dzl) % NZL)
        for x in range(NX)
        for z in range(NZL)
    ]


def col_perm(dy, dzh, dcore):
    return [
        (
            (y * NZH + z) * NCORE + k,
            (((y + dy) % NY) * NZH + (z + dzh) % NZH) * NCORE + (k + dcore) % NCORE,
        )
        for y in range(NY)
        for z in range(NZH)
        for k in range(NCORE)
    ]


def split3(value):
    high = lax.reduce_precision(value, 8, 7)
    rest = value - high
    mid = lax.reduce_precision(rest, 8, 7)
    low = rest - mid
    return [part.astype(jnp.bfloat16) for part in (high, mid, low)]


def segment_table(segment, prefix):
    ids = jnp.arange(SEGMENTS, dtype=jnp.int32)
    start = jnp.sum((segment[None, :] < ids[:, None]).astype(jnp.int32), axis=1)
    finish = jnp.sum((segment[None, :] <= ids[:, None]).astype(jnp.int32), axis=1)
    owner = jnp.max(jnp.where(segment[None, :] == ids[:, None], prefix[None, :], 0), axis=1)
    picked = owner[:, None] == ids[None, :]
    low = jnp.sum(jnp.where(picked, start[None, :], 0), axis=1)
    high = jnp.sum(jnp.where(picked, finish[None, :], 0), axis=1)
    return jnp.stack([start, low, high])


def attention_kernel(
    jcount,
    ids_ref,
    table_ref,
    list_ref,
    count_ref,
    pay0,
    pay1,
    pay2,
    pay3,
    kv0,
    kv1,
    dq0,
    dq1,
    dq2,
    dq3,
    dkv_ref,
    k_scr,
    v_scr,
    kt_scr,
    dk_scr,
    dv_scr,
    lse_scr,
    delta_scr,
    q_scr,
    do_scr,
    qt_scr,
    dot_scr,
    dqt_scr,
):
    f32, bf16 = jnp.float32, jnp.bfloat16
    pays = (pay0, pay1, pay2, pay3)
    dqs = (dq0, dq1, dq2, dq3)
    rows = jcount * 32
    scale = 128.0 ** -0.5
    my_x, my_zl, my_c = ids_ref[0], ids_ref[1], ids_ref[2]
    my_y, my_zh, my_core, my_g = ids_ref[3], ids_ref[4], ids_ref[5], ids_ref[6]

    dk_scr[...] = jnp.zeros_like(dk_scr)
    dv_scr[...] = jnp.zeros_like(dv_scr)

    def prepare(slot, _):
        for half, ref in enumerate((kv0, kv1)):
            key = ref[slot, 0]
            k_scr[half * 16 + slot] = key
            v_scr[half * 16 + slot] = ref[slot, 1]
            kt_scr[half * 16 + slot] = key.T
        return 0

    lax.fori_loop(0, 16, prepare, 0)

    for xs in range(NX):
        terms = [
            pays[xs][pl.ds(8 * rows + part * 16, 16), :].astype(f32) for part in range(6)
        ]
        lanes = pl.ds(xs * 128, 128)
        lse_scr[:, lanes] = (terms[0] + terms[1] + terms[2]) * LOG2E
        delta_scr[:, lanes] = terms[3] + terms[4] + terms[5]

    lane = lax.broadcasted_iota(jnp.int32, (1, 512), 1)
    row_of = ((my_x + (lane >> 7)) & 3) * 4 + ((my_zl + (lane >> 5)) & 3)
    row_off = row_of * 8 + (lane & 7)
    key_iota = lax.broadcasted_iota(jnp.int32, (128, 512), 0)

    def query_block(j, _):
        count = count_ref[j]
        base = (j * 32 + my_c) * 128

        @pl.when(count == 0)
        def _():
            for xs in range(NX):
                for zs in range(NZL):
                    dqs[xs][pl.ds(zs * rows + j * 32, 32), :] = jnp.zeros((32, 128), bf16)

        @pl.when(count > 0)
        def _():
            for xs in range(NX):
                for zs in range(NZL):
                    at = (xs * NZL + zs) * 32
                    q_scr[pl.ds(at, 32), :] = pays[xs][pl.ds(zs * rows + j * 32, 32), :]
                    do_scr[pl.ds(at, 32), :] = pays[xs][
                        pl.ds((NZL + zs) * rows + j * 32, 32), :
                    ]
            qt_scr[...] = q_scr[...].T
            dot_scr[...] = do_scr[...].T
            dqt_scr[...] = jnp.zeros_like(dqt_scr)

            place = base + row_off
            own_low = jnp.zeros_like(place)
            pre_low = jnp.zeros_like(place)
            pre_high = jnp.zeros_like(place)
            first_low, last_low = jnp.int32(0), jnp.int32(0)
            tile_low, tile_high = jnp.int32(0), jnp.int32(0)
            for s in range(SEGMENTS):
                start, low, high = table_ref[0, s], table_ref[1, s], table_ref[2, s]
                here = place >= start
                own_low = jnp.where(here, start, own_low)
                pre_low = jnp.where(here, low, pre_low)
                pre_high = jnp.where(here, high, pre_high)
                first_low = jnp.where(base >= start, start, first_low)
                tile_low = jnp.where(base >= start, low, tile_low)
                tile_high = jnp.where(base >= start, high, tile_high)
                last_low = jnp.where(base + 127 >= start, start, last_low)
            pre_high = jnp.minimum(pre_high, place + 1)
            single = first_low == last_low
            tile_high = jnp.where(single, jnp.minimum(tile_high, base + 1), 0)
            lse_row = lse_scr[pl.ds(j, 1), :]
            delta_row = delta_scr[pl.ds(j, 1), :]

            def one(m, masked):
                slots, firsts = [], []
                for u in range(2):
                    at = 2 * m + u
                    key_id = list_ref[j, jnp.minimum(at, 31)]
                    slot = (
                        ((key_id & 1) ^ my_core) * 16
                        + (((key_id >> 3) - my_y) & 3) * 4
                        + (((key_id >> 1) - my_zh) & 3)
                    )
                    slots.append(slot)
                    firsts.append(jnp.where(at < count, (my_g * 32 + key_id) * 128, NEVER))
                pbs, dsbs = [], []
                for u in range(2):
                    scores = jnp.dot(
                        k_scr[slots[u]], qt_scr[...], preferred_element_type=f32
                    )
                    weights = jnp.exp2(scores * (scale * LOG2E) - lse_row)
                    if masked:
                        key_at = key_iota + firsts[u]
                        allowed = ((key_at >= own_low) & (key_at <= place)) | (
                            (key_at >= pre_low) & (key_at < pre_high)
                        )
                        weights = jnp.where(allowed, weights, 0.0)
                    weight_grad = jnp.dot(
                        v_scr[slots[u]], dot_scr[...], preferred_element_type=f32
                    )
                    score_grad = weights * (weight_grad - delta_row)
                    pb = weights.astype(bf16)
                    dsb = score_grad.astype(bf16)
                    dv_scr[slots[u]] += jnp.dot(pb, do_scr[...], preferred_element_type=f32)
                    dk_scr[slots[u]] += jnp.dot(dsb, q_scr[...], preferred_element_type=f32)
                    dsbs.append(dsb)
                keys_t = jnp.concatenate([kt_scr[slots[0]], kt_scr[slots[1]]], axis=1)
                dqt_scr[...] += jnp.dot(
                    keys_t, jnp.concatenate(dsbs, axis=0), preferred_element_type=f32
                )

            def step(m, _):
                full = 2 * m + 1 < count
                for u in range(2):
                    key_id = list_ref[j, jnp.minimum(2 * m + u, 31)]
                    first = (my_g * 32 + key_id) * 128
                    own = (first >= last_low) & (first + 127 <= base)
                    pre = (first >= tile_low) & (first + 128 <= tile_high)
                    full = full & (own | pre)

                @pl.when(full)
                def _():
                    one(m, False)

                @pl.when(jnp.logical_not(full))
                def _():
                    one(m, True)

                return 0

            lax.fori_loop(0, (count + 1) // 2, step, 0)
            dq = (dqt_scr[...] * scale).astype(bf16).T
            for xs in range(NX):
                for zs in range(NZL):
                    at = (xs * NZL + zs) * 32
                    dqs[xs][pl.ds(zs * rows + j * 32, 32), :] = dq[at : at + 32]

        return 0

    lax.fori_loop(0, jcount, query_block, 0)

    def finish(slot, _):
        for half in range(2):
            dkv_ref[half, slot, 0] = (dk_scr[half * 16 + slot] * scale).astype(bf16)
            dkv_ref[half, slot, 1] = dv_scr[half * 16 + slot].astype(bf16)
        return 0

    lax.fori_loop(0, 16, finish, 0)


def run_attention(ids, table, lists, counts, pays, kv0, kv1, jcount):
    f32, bf16 = jnp.float32, jnp.bfloat16
    rows = jcount * 32
    smem = pl.BlockSpec(memory_space=pltpu.SMEM)
    vmem = pl.BlockSpec(memory_space=pltpu.VMEM)
    part = jax.ShapeDtypeStruct((NZL * rows, 128), bf16)
    return pl.pallas_call(
        functools.partial(attention_kernel, jcount),
        out_shape=[part] * 4 + [jax.ShapeDtypeStruct((2, 16, 2, 128, 128), bf16)],
        in_specs=[smem] * 4 + [vmem] * 6,
        out_specs=[vmem] * 5,
        scratch_shapes=[
            pltpu.VMEM((32, 128, 128), bf16),
            pltpu.VMEM((32, 128, 128), bf16),
            pltpu.VMEM((32, 128, 128), bf16),
            pltpu.VMEM((32, 128, 128), f32),
            pltpu.VMEM((32, 128, 128), f32),
            pltpu.VMEM((16, 512), f32),
            pltpu.VMEM((16, 512), f32),
            pltpu.VMEM((512, 128), bf16),
            pltpu.VMEM((512, 128), bf16),
            pltpu.VMEM((128, 512), bf16),
            pltpu.VMEM((128, 512), bf16),
            pltpu.VMEM((128, 512), f32),
        ],
        compiler_params=pltpu.CompilerParams(vmem_limit_bytes=48 * 1024 * 1024),
        name="attention_backward",
    )(ids, table, lists, counts, *pays, kv0, kv1)


def total(parts):
    out = parts[0].astype(jnp.float32)
    for part in parts[1:]:
        out = out + part.astype(jnp.float32)
    return out.astype(jnp.bfloat16)


def on_device(
    queries,
    grad_output,
    attn_output,
    key_states,
    value_states,
    log_sum,
    segment,
    prefix,
    block_list,
    block_count,
):
    jcount = queries.shape[0]
    rows = jcount * 32
    row = lax.axis_index("row")
    col = lax.axis_index("col")
    my_x, my_zl = row // NZL, row % NZL
    my_y, my_zh, my_core = col // (NZH * NCORE), (col // NCORE) % NZH, col % NCORE
    ids = jnp.stack([my_x, my_zl, col, my_y, my_zh, my_core, row]).astype(jnp.int32)

    def heads_first(value):
        return value.reshape(jcount, 8, 4, 128).transpose(0, 2, 1, 3).reshape(rows, 128)

    with jax.named_scope("pack"):
        delta = jnp.sum(
            (grad_output.astype(jnp.float32) * attn_output.astype(jnp.float32)).reshape(
                jcount, 8, 4, 128
            ),
            axis=3,
        )
        lse = log_sum.reshape(jcount, 8, 4)
        aux = jnp.stack(
            split3(lse.transpose(0, 2, 1).reshape(jcount, 32))
            + split3(delta.transpose(0, 2, 1).reshape(jcount, 32))
        )
        payload = jnp.concatenate(
            [heads_first(queries), heads_first(grad_output), aux.reshape(-1, 128)], axis=0
        )
        pair = jnp.stack([key_states, value_states])

    with jax.named_scope("gather_kv_zh"):
        kv = jnp.stack(
            [pair] + [lax.ppermute(pair, "col", col_perm(0, -s, 0)) for s in range(1, NZH)]
        )
    with jax.named_scope("gather_q_zl"):
        got = [payload] + [
            lax.ppermute(payload, "row", row_perm(0, -s)) for s in range(1, NZL)
        ]
        wide = jnp.concatenate(
            [part[:rows] for part in got]
            + [part[rows : 2 * rows] for part in got]
            + [
                jnp.concatenate(
                    [part[2 * rows :].reshape(6, jcount, 32) for part in got], axis=2
                ).reshape(6 * jcount, 128)
            ],
            axis=0,
        )
    with jax.named_scope("gather_kv_y"):
        kv = jnp.stack(
            [kv] + [lax.ppermute(kv, "col", col_perm(-s, 0, 0)) for s in range(1, NY)]
        ).reshape(NY * NZH, 2, 128, 128)
    with jax.named_scope("gather_kv_core"):
        kv_other = lax.ppermute(kv, "col", col_perm(0, 0, 1))
    with jax.named_scope("gather_q_x"):
        pays = [wide] + [lax.ppermute(wide, "row", row_perm(-s, 0)) for s in range(1, NX)]

    table = segment_table(segment, prefix)
    *dqs, dkv = run_attention(
        ids, table, block_list[:, 0, 0, :], block_count[:, 0, 0], pays, kv, kv_other, jcount
    )

    with jax.named_scope("scatter_kv_core"):
        mine = total([dkv[0], lax.ppermute(dkv[1], "col", col_perm(0, 0, 1))])
        mine = mine.reshape(NY, NZH, 2, 128, 128)
    with jax.named_scope("scatter_q_x"):
        dq = total(
            [dqs[0]] + [lax.ppermute(dqs[s], "row", row_perm(s, 0)) for s in range(1, NX)]
        ).reshape(NZL, rows, 128)
    with jax.named_scope("scatter_kv_y"):
        mine = total(
            [mine[0]] + [lax.ppermute(mine[s], "col", col_perm(s, 0, 0)) for s in range(1, NY)]
        )
    with jax.named_scope("scatter_q_zl"):
        dq = total(
            [dq[0]] + [lax.ppermute(dq[s], "row", row_perm(0, s)) for s in range(1, NZL)]
        )
    with jax.named_scope("scatter_kv_zh"):
        mine = total(
            [mine[0]] + [lax.ppermute(mine[s], "col", col_perm(0, s, 0)) for s in range(1, NZH)]
        )
    dq = dq.reshape(jcount, 4, 8, 128).transpose(0, 2, 1, 3).reshape(jcount, 1, 8, 512)
    return dq, mine[0], mine[1]


def solution(mesh):
    in_specs = (
        P(None, "col", "row", None),
        P(None, "col", "row", None),
        P(None, "col", "row", None),
        P(("row", "col"), None),
        P(("row", "col"), None),
        P(None, "col", "row", None),
        P(),
        P(),
        P(None, "col", "row", None),
        P(None, "col", "row"),
    )
    out_specs = (P(None, "col", "row", None), P(("row", "col"), None), P(("row", "col"), None))
    return jax.shard_map(
        on_device, mesh=mesh, in_specs=in_specs, out_specs=out_specs, check_vma=False
    )
```

profile of v0, /device:TPU:58, one launch (start us, length us, event | category | flops | bytes accessed | tf_op | source)
XLA Modules:
  0.0 243.7 jit_solution(22387611429355215)
XLA Ops:
  0.6 0.0 copy-start.4
  0.6 0.8 fusion.6
  1.5 14.8 %collective-permute-start.7 = (bf16[2,128,128]{2,1,0:T(8,128)(2,1)S(1)}, bf16[2,128,128]{2,1,0:T(8,128)(2,1)S(1)}, u32[]{:S(2)}, u32[]{:S(2)}) collective-permute-start(bf16[2,128,128]{2,1,0:T(8,128)(2,1)S(1)} %get-tuple-element.32), channel_id=1, source_target_pairs={{0,4},{1,5},{2,6},{3,7},{4,0},{5,1},{6,2},{7,3},{8,12},{9,13},{10,... | collective-permute-start | bytes 196616 | tf_op jit(solution)/shard_map/gather_kv_zh/ppermute | solution.py:320
  16.3 1.1 bitcast_reduce_fusion
  17.4 0.1 copy.21
  17.5 0.7 constant_dynamic-update-slice_fusion.5
  18.2 0.7 constant_dynamic-update-slice_fusion.4
  19.0 0.7 constant_dynamic-update-slice_fusion.3
  19.7 0.1 copy.22
  19.8 0.1 reshape.178
  19.9 1.0 pad_maximum_fusion.1
  20.9 0.0 copy-start.3
  20.9 3.1 %collective-permute-start.2 = (bf16[1048,128]{1,0:T(8,128)(2,1)S(1)}, bf16[1048,128]{1,0:T(8,128)(2,1)S(1)}, u32[]{:S(2)}, u32[]{:S(2)}) collective-permute-start(bf16[1048,128]{1,0:T(8,128)(2,1)S(1)} %pad_maximum_fusion.1), channel_id=1, source_target_pairs={{0,32},{32,64},{64,96},{96,0},{128,160},{160,192},{192,224},{224,1... | collective-permute-start | bytes 804872 | tf_op jit(solution)/shard_map/gather_q_zl/ppermute | solution.py:324
  24.0 4.3 %collective-permute-start.1 = (bf16[1048,128]{1,0:T(8,128)(2,1)S(1)}, bf16[1048,128]{1,0:T(8,128)(2,1)S(1)}, u32[]{:S(2)}, u32[]{:S(2)}) collective-permute-start(bf16[1048,128]{1,0:T(8,128)(2,1)S(1)} %pad_maximum_fusion.1), channel_id=1, source_target_pairs={{0,64},{32,96},{64,0},{96,32},{128,192},{160,224},{192,128},{224,1... | collective-permute-start | bytes 804872 | tf_op jit(solution)/shard_map/gather_q_zl/ppermute | solution.py:324
  28.3 2.0 collective-permute-start
  30.3 3.3 %collective-permute-start.6 = (bf16[2,128,128]{2,1,0:T(8,128)(2,1)S(1)}, bf16[2,128,128]{2,1,0:T(8,128)(2,1)S(1)}, u32[]{:S(2)}, u32[]{:S(2)}) collective-permute-start(bf16[2,128,128]{2,1,0:T(8,128)(2,1)S(1)} %get-tuple-element.32), channel_id=1, source_target_pairs={{0,6},{1,7},{2,0},{3,1},{4,2},{5,3},{6,4},{7,5},{8,14},{9,15},{10,... | collective-permute-start | bytes 196616 | tf_op jit(solution)/shard_map/gather_kv_zh/ppermute | solution.py:320
  33.7 0.0 collective-permute-done.7
  33.7 6.4 %collective-permute-start.8 = (bf16[2,128,128]{2,1,0:T(8,128)(2,1)S(1)}, bf16[2,128,128]{2,1,0:T(8,128)(2,1)S(1)}, u32[]{:S(2)}, u32[]{:S(2)}) collective-permute-start(bf16[2,128,128]{2,1,0:T(8,128)(2,1)S(1)} %get-tuple-element.32), channel_id=1, source_target_pairs={{0,2},{1,3},{2,4},{3,5},{4,6},{5,7},{6,0},{7,1},{8,10},{9,11},{10,... | collective-permute-start | bytes 196616 | tf_op jit(solution)/shard_map/gather_kv_zh/ppermute | solution.py:320
  40.1 8.9 %collective-permute-done.6 = bf16[2,128,128]{2,1,0:T(8,128)(2,1)S(1)} collective-permute-done((bf16[2,128,128]{2,1,0:T(8,128)(2,1)S(1)}, bf16[2,128,128]{2,1,0:T(8,128)(2,1)S(1)}, u32[]{:S(2)}, u32[]{:S(2)}) %collective-permute-start.6) | collective-permute-done | bytes 65568 | tf_op jit(solution)/shard_map/gather_kv_zh/ppermute | solution.py:320
  49.0 4.2 %collective-permute-done.8 = bf16[2,128,128]{2,1,0:T(8,128)(2,1)S(1)} collective-permute-done((bf16[2,128,128]{2,1,0:T(8,128)(2,1)S(1)}, bf16[2,128,128]{2,1,0:T(8,128)(2,1)S(1)}, u32[]{:S(2)}, u32[]{:S(2)}) %collective-permute-start.8) | collective-permute-done | bytes 65568 | tf_op jit(solution)/shard_map/gather_kv_zh/ppermute | solution.py:320
  53.3 3.1 %collective-permute-start.10 = (bf16[4,2,128,128]{3,2,1,0:T(8,128)(2,1)S(1)}, bf16[4,2,128,128]{3,2,1,0:T(8,128)(2,1)S(1)}, u32[]{:S(2)}, u32[]{:S(2)}) collective-permute-start(bf16[4,2,128,128]{3,2,1,0:T(8,128)(2,1)S(1)} %get-tuple-element.28), channel_id=1, source_target_pairs={{0,16},{1,17},{2,18},{3,19},{4,20},{5,21},{6,22},{7,23},{8,24},{9,... | collective-permute-start | bytes 786440 | tf_op jit(solution)/shard_map/gather_kv_y/ppermute | solution.py:338
  56.5 1.9 collective-permute-start.9
  58.4 5.1 %collective-permute-start.11 = (bf16[4,2,128,128]{3,2,1,0:T(8,128)(2,1)S(1)}, bf16[4,2,128,128]{3,2,1,0:T(8,128)(2,1)}, u32[]{:S(2)}, u32[]{:S(2)}) collective-permute-start(bf16[4,2,128,128]{3,2,1,0:T(8,128)(2,1)S(1)} %get-tuple-element.28), channel_id=1, source_target_pairs={{0,8},{1,9},{2,10},{3,11},{4,12},{5,13},{6,14},{7,15},{8,16},{9,17... | collective-permute-start | bytes 786440 | tf_op jit(solution)/shard_map/gather_kv_y/ppermute | solution.py:338
  63.5 0.1 concatenate.22
  63.6 0.0 collective-permute-done.1
  63.6 0.1 concatenate.21
  63.7 0.0 collective-permute-done
  63.7 0.1 concatenate.20
  64.0 0.1 constant_dynamic-update-slice_fusion.6.pay0
  64.1 3.4 %collective-permute-start.5 = (bf16[4192,128]{1,0:T(8,128)(2,1)S(1)}, bf16[4192,128]{1,0:T(8,128)(2,1)}, u32[]{:S(2)}, u32[]{:S(2)}) collective-permute-start(bf16[4192,128]{1,0:T(8,128)(2,1)S(1)} %constant_dynamic-update-slice_fusion.6.pay0), channel_id=1, source_target_pairs={{0,128},{32,160},{64,192},{96,224},{128,256},{160,288},{192,320},{... | collective-permute-start | bytes 3219464 | tf_op jit(solution)/shard_map/gather_q_x/ppermute | solution.py:343
  67.5 3.0 %collective-permute-start.4 = (bf16[4192,128]{1,0:T(8,128)(2,1)S(1)}, bf16[4192,128]{1,0:T(8,128)(2,1)}, u32[]{:S(2)}, u32[]{:S(2)}) collective-permute-start(bf16[4192,128]{1,0:T(8,128)(2,1)S(1)} %constant_dynamic-update-slice_fusion.6.pay0), channel_id=1, source_target_pairs={{0,256},{32,288},{64,320},{96,352},{128,384},{160,416},{192,448},{... | collective-permute-start | bytes 3219464 | tf_op jit(solution)/shard_map/gather_q_x/ppermute | solution.py:343
  70.6 4.1 %collective-permute-start.3 = (bf16[4192,128]{1,0:T(8,128)(2,1)S(1)}, bf16[4192,128]{1,0:T(8,128)(2,1)}, u32[]{:S(2)}, u32[]{:S(2)}) collective-permute-start(bf16[4192,128]{1,0:T(8,128)(2,1)S(1)} %constant_dynamic-update-slice_fusion.6.pay0), channel_id=1, source_target_pairs={{0,384},{32,416},{64,448},{96,480},{128,0},{160,32},{192,64},{224,... | collective-permute-start | bytes 3219464 | tf_op jit(solution)/shard_map/gather_q_x/ppermute | solution.py:343
  74.7 0.7 copy-done.7
  75.4 1.3 pad_maximum_fusion
  76.7 1.9 collective-permute-start.12
  78.6 0.1 stack.91.ids_ref
  78.7 2.7 %convert_reduce_fusion.1 = (s32[11]{0:T(128)S(1)}, s32[11]{0:T(128)S(1)}, s32[11]{0:T(128)S(1)}) fusion(s32[65536]{0:T(1024)S(1)} %copy-done.5, s32[65536]{0:T(1024)} %param.17), kind=kLoop, calls=%fused_computation.4 | loop fusion | flops 6488031 | bytes 524420 | tf_op jit(solution)/shard_map/reduce_sum | solution.py:46
  81.4 0.2 select_reduce_fusion.2
  81.6 11.1 %collective-permute-done.5.pay3 = bf16[4192,128]{1,0:T(8,128)(2,1)} collective-permute-done((bf16[4192,128]{1,0:T(8,128)(2,1)S(1)}, bf16[4192,128]{1,0:T(8,128)(2,1)}, u32[]{:S(2)}, u32[]{:S(2)}) %collective-permute-start.5) | collective-permute-done | bytes 1073184 | tf_op jit(solution)/shard_map/gather_q_x/ppermute | solution.py:343
  92.8 4.9 %collective-permute-done.4.pay2 = bf16[4192,128]{1,0:T(8,128)(2,1)} collective-permute-done((bf16[4192,128]{1,0:T(8,128)(2,1)S(1)}, bf16[4192,128]{1,0:T(8,128)(2,1)}, u32[]{:S(2)}, u32[]{:S(2)}) %collective-permute-start.4) | collective-permute-done | bytes 1073184 | tf_op jit(solution)/shard_map/gather_q_x/ppermute | solution.py:343
  97.7 19.1 %collective-permute-done.3.pay1 = bf16[4192,128]{1,0:T(8,128)(2,1)} collective-permute-done((bf16[4192,128]{1,0:T(8,128)(2,1)S(1)}, bf16[4192,128]{1,0:T(8,128)(2,1)}, u32[]{:S(2)}, u32[]{:S(2)}) %collective-permute-start.3) | collective-permute-done | bytes 1073184 | tf_op jit(solution)/shard_map/gather_q_x/ppermute | solution.py:343
  116.8 24.6 %attention_backward.1 = (bf16[2048,128]{1,0:T(8,128)(2,1)S(1)}, bf16[2048,128]{1,0:T(8,128)(2,1)S(1)}, bf16[2048,128]{1,0:T(8,128)(2,1)S(1)}, bf16[2048,128]{1,0:T(8,128)(2,1)S(1)}, bf16[2,16,2,128,128]{4,3,2,1,0:T(8,128)(2,1)}) custom-call(s32[7]{0:T(128)S(1)} %stack.91.ids_ref, s32[3,11]{1,0:T(4,128)S(1)} %pad_add_fusion.table_ref, s32[16,32]{1,0:T(8,128)S(1)} %bitcast.95, ...), custom_call_target="tpu_custom_call" | custom-call | tf_op jit(solution)/shard_map/attention_backward/pallas_call | solution.py:247
  141.5 1.4 slice_bitcast_fusion
  142.9 2.6 %collective-permute-start.19 = (bf16[16,2,128,128]{3,2,1,0:T(8,128)(2,1)S(1)}, bf16[16,2,128,128]{3,2,1,0:T(8,128)(2,1)S(1)}, u32[]{:S(2)}, u32[]{:S(2)}) collective-permute-start(bf16[16,2,128,128]{3,2,1,0:T(8,128)(2,1)S(1)} %slice_bitcast_fusion), channel_id=1, source_target_pairs={{0,1},{1,0},{2,3},{3,2},{4,5},{5,4},{6,7},{7,6},{8,9},{9,8},{10,11... | collective-permute-start | bytes 3145736 | tf_op jit(solution)/shard_map/scatter_kv_core/ppermute | solution.py:351
  145.5 1.9 collective-permute-start.13
  147.4 13.5 %collective-permute-start.14 = (bf16[2048,128]{1,0:T(8,128)(2,1)S(1)}, bf16[2048,128]{1,0:T(8,128)(2,1)S(1)}, u32[]{:S(2)}, u32[]{:S(2)}) collective-permute-start(bf16[2048,128]{1,0:T(8,128)(2,1)S(1)} %get-tuple-element.10), channel_id=1, source_target_pairs={{0,256},{32,288},{64,320},{96,352},{128,384},{160,416},{192,448},{... | collective-permute-start | bytes 1572872 | tf_op jit(solution)/shard_map/scatter_q_x/ppermute | solution.py:355
  160.9 3.9 %collective-permute-start.15 = (bf16[2048,128]{1,0:T(8,128)(2,1)S(1)}, bf16[2048,128]{1,0:T(8,128)(2,1)S(1)}, u32[]{:S(2)}, u32[]{:S(2)}) collective-permute-start(bf16[2048,128]{1,0:T(8,128)(2,1)S(1)} %get-tuple-element.11), channel_id=1, source_target_pairs={{0,384},{32,416},{64,448},{96,480},{128,0},{160,32},{192,64},{224,... | collective-permute-start | bytes 1572872 | tf_op jit(solution)/shard_map/scatter_q_x/ppermute | solution.py:355
  164.8 0.4 fusion
  165.2 0.1 fusion.8
  165.3 3.6 %collective-permute-start.20 = (bf16[4,2,128,128]{3,2,1,0:T(8,128)(2,1)S(1)}, bf16[4,2,128,128]{3,2,1,0:T(8,128)(2,1)S(1)}, u32[]{:S(2)}, u32[]{:S(2)}) collective-permute-start(bf16[4,2,128,128]{3,2,1,0:T(8,128)(2,1)S(1)} %get-tuple-element.18), channel_id=1, source_target_pairs={{0,8},{1,9},{2,10},{3,11},{4,12},{5,13},{6,14},{7,15},{8,16},{9,17... | collective-permute-start | bytes 786440 | tf_op jit(solution)/shard_map/scatter_kv_y/ppermute | solution.py:359
  168.9 2.2 collective-permute-start.22
  171.1 9.9 %collective-permute-start.21 = (bf16[4,2,128,128]{3,2,1,0:T(8,128)(2,1)S(1)}, bf16[4,2,128,128]{3,2,1,0:T(8,128)(2,1)S(1)}, u32[]{:S(2)}, u32[]{:S(2)}) collective-permute-start(bf16[4,2,128,128]{3,2,1,0:T(8,128)(2,1)S(1)} %get-tuple-element.20), channel_id=1, source_target_pairs={{0,16},{1,17},{2,18},{3,19},{4,20},{5,21},{6,22},{7,23},{8,24},{9,... | collective-permute-start | bytes 786440 | tf_op jit(solution)/shard_map/scatter_kv_y/ppermute | solution.py:359
  181.1 3.3 %collective-permute-done.15 = bf16[2048,128]{1,0:T(8,128)(2,1)S(1)} collective-permute-done((bf16[2048,128]{1,0:T(8,128)(2,1)S(1)}, bf16[2048,128]{1,0:T(8,128)(2,1)S(1)}, u32[]{:S(2)}, u32[]{:S(2)}) %collective-permute-start.15) | collective-permute-done | bytes 524320 | tf_op jit(solution)/shard_map/scatter_q_x/ppermute | solution.py:355
  184.4 0.3 add_convert_fusion
  184.7 1.9 collective-permute-start.16
  186.6 5.3 %collective-permute-start.18 = (bf16[512,128]{1,0:T(8,128)(2,1)S(1)}, bf16[512,128]{1,0:T(8,128)(2,1)S(1)}, u32[]{:S(2)}, u32[]{:S(2)}) collective-permute-start(bf16[512,128]{1,0:T(8,128)(2,1)S(1)} %get-tuple-element.22), channel_id=1, source_target_pairs={{0,96},{32,0},{64,32},{96,64},{128,224},{160,128},{192,160},{224,1... | collective-permute-start | bytes 393224 | tf_op jit(solution)/shard_map/scatter_q_zl/ppermute | solution.py:363
  191.9 20.7 %collective-permute-start.17 = (bf16[512,128]{1,0:T(8,128)(2,1)S(1)}, bf16[512,128]{1,0:T(8,128)(2,1)S(1)}, u32[]{:S(2)}, u32[]{:S(2)}) collective-permute-start(bf16[512,128]{1,0:T(8,128)(2,1)S(1)} %get-tuple-element.23), channel_id=1, source_target_pairs={{0,64},{32,96},{64,0},{96,32},{128,192},{160,224},{192,128},{224,1... | collective-permute-start | bytes 393224 | tf_op jit(solution)/shard_map/scatter_q_zl/ppermute | solution.py:363
  212.7 0.1 add_convert_fusion.1
  212.8 3.0 %collective-permute-start.23 = (bf16[2,128,128]{2,1,0:T(8,128)(2,1)S(1)}, bf16[2,128,128]{2,1,0:T(8,128)(2,1)S(1)}, u32[]{:S(2)}, u32[]{:S(2)}) collective-permute-start(bf16[2,128,128]{2,1,0:T(8,128)(2,1)S(1)} %get-tuple-element.24), channel_id=1, source_target_pairs={{0,2},{1,3},{2,4},{3,5},{4,6},{5,7},{6,0},{7,1},{8,10},{9,11},{10,... | collective-permute-start | bytes 196616 | tf_op jit(solution)/shard_map/scatter_kv_zh/ppermute | solution.py:367
  215.8 6.8 %collective-permute-start.25 = (bf16[2,128,128]{2,1,0:T(8,128)(2,1)S(1)}, bf16[2,128,128]{2,1,0:T(8,128)(2,1)S(1)}, u32[]{:S(2)}, u32[]{:S(2)}) collective-permute-start(bf16[2,128,128]{2,1,0:T(8,128)(2,1)S(1)} %get-tuple-element.25), channel_id=1, source_target_pairs={{0,6},{1,7},{2,0},{3,1},{4,2},{5,3},{6,4},{7,5},{8,14},{9,15},{10,... | collective-permute-start | bytes 196616 | tf_op jit(solution)/shard_map/scatter_kv_zh/ppermute | solution.py:367
  222.6 12.5 %collective-permute-start.24 = (bf16[2,128,128]{2,1,0:T(8,128)(2,1)S(1)}, bf16[2,128,128]{2,1,0:T(8,128)(2,1)S(1)}, u32[]{:S(2)}, u32[]{:S(2)}) collective-permute-start(bf16[2,128,128]{2,1,0:T(8,128)(2,1)S(1)} %get-tuple-element.26), channel_id=1, source_target_pairs={{0,4},{1,5},{2,6},{3,7},{4,0},{5,1},{6,2},{7,3},{8,12},{9,13},{10,... | collective-permute-start | bytes 196616 | tf_op jit(solution)/shard_map/scatter_kv_zh/ppermute | solution.py:367
  235.1 0.7 add_convert_fusion.2
  235.9 7.1 %collective-permute-done.24 = bf16[2,128,128]{2,1,0:T(8,128)(2,1)S(1)} collective-permute-done((bf16[2,128,128]{2,1,0:T(8,128)(2,1)S(1)}, bf16[2,128,128]{2,1,0:T(8,128)(2,1)S(1)}, u32[]{:S(2)}, u32[]{:S(2)}) %collective-permute-start.24) | collective-permute-done | bytes 65568 | tf_op jit(solution)/shard_map/scatter_kv_zh/ppermute | solution.py:367
  243.0 0.6 slice_bitcast_fusion.5
  (48 shorter events, 0.4 us)
Async XLA Ops:
  0.6 39.4 %copy-start.4 = (bf16[16,1,8,512]{3,2,1,0:T(8,128)(2,1)S(1)}, bf16[16,1,8,512]{3,2,1,0:T(8,128)(2,1)}, u32[]{:S(2)}) copy-start(bf16[16,1,8,512]{3,2,1,0:T(8,128)(2,1)} %param.10) | copy-start | bytes 393220
  1.5 32.2 %collective-permute-start.7 = (bf16[2,128,128]{2,1,0:T(8,128)(2,1)S(1)}, bf16[2,128,128]{2,1,0:T(8,128)(2,1)S(1)}, u32[]{:S(2)}, u32[]{:S(2)}) collective-permute-start(bf16[2,128,128]{2,1,0:T(8,128)(2,1)S(1)} %get-tuple-element.32), channel_id=1, source_target_pairs={{0,4},{1,5},{2,6},{3,7},{4,0},{5,1},{6,2},{7,3},{8,12},{9,13},{10,... | collective-permute-start | bytes 196616 | tf_op jit(solution)/shard_map/gather_kv_zh/ppermute | solution.py:320
  20.9 43.0 %copy-start.3 = (bf16[16,1,8,512]{3,2,1,0:T(8,128)(2,1)S(1)}, bf16[16,1,8,512]{3,2,1,0:T(8,128)(2,1)}, u32[]{:S(2)}) copy-start(bf16[16,1,8,512]{3,2,1,0:T(8,128)(2,1)} %param.11) | copy-start | bytes 393220
  20.9 37.5 %collective-permute-start.2 = (bf16[1048,128]{1,0:T(8,128)(2,1)S(1)}, bf16[1048,128]{1,0:T(8,128)(2,1)S(1)}, u32[]{:S(2)}, u32[]{:S(2)}) collective-permute-start(bf16[1048,128]{1,0:T(8,128)(2,1)S(1)} %pad_maximum_fusion.1), channel_id=1, source_target_pairs={{0,32},{32,64},{64,96},{96,0},{128,160},{160,192},{192,224},{224,1... | collective-permute-start | bytes 804872 | tf_op jit(solution)/shard_map/gather_q_zl/ppermute | solution.py:324
  24.0 39.6 %collective-permute-start.1 = (bf16[1048,128]{1,0:T(8,128)(2,1)S(1)}, bf16[1048,128]{1,0:T(8,128)(2,1)S(1)}, u32[]{:S(2)}, u32[]{:S(2)}) collective-permute-start(bf16[1048,128]{1,0:T(8,128)(2,1)S(1)} %pad_maximum_fusion.1), channel_id=1, source_target_pairs={{0,64},{32,96},{64,0},{96,32},{128,192},{160,224},{192,128},{224,1... | collective-permute-start | bytes 804872 | tf_op jit(solution)/shard_map/gather_q_zl/ppermute | solution.py:324
  28.3 35.5 %collective-permute-start = (bf16[1048,128]{1,0:T(8,128)(2,1)S(1)}, bf16[1048,128]{1,0:T(8,128)(2,1)S(1)}, u32[]{:S(2)}, u32[]{:S(2)}) collective-permute-start(bf16[1048,128]{1,0:T(8,128)(2,1)S(1)} %pad_maximum_fusion.1), channel_id=1, source_target_pairs={{0,96},{32,0},{64,32},{96,64},{128,224},{160,128},{192,160},{224,1... | collective-permute-start | bytes 804872 | tf_op jit(solution)/shard_map/gather_q_zl/ppermute | solution.py:324
  30.3 18.7 %collective-permute-start.6 = (bf16[2,128,128]{2,1,0:T(8,128)(2,1)S(1)}, bf16[2,128,128]{2,1,0:T(8,128)(2,1)S(1)}, u32[]{:S(2)}, u32[]{:S(2)}) collective-permute-start(bf16[2,128,128]{2,1,0:T(8,128)(2,1)S(1)} %get-tuple-element.32), channel_id=1, source_target_pairs={{0,6},{1,7},{2,0},{3,1},{4,2},{5,3},{6,4},{7,5},{8,14},{9,15},{10,... | collective-permute-start | bytes 196616 | tf_op jit(solution)/shard_map/gather_kv_zh/ppermute | solution.py:320
  33.7 19.6 %collective-permute-start.8 = (bf16[2,128,128]{2,1,0:T(8,128)(2,1)S(1)}, bf16[2,128,128]{2,1,0:T(8,128)(2,1)S(1)}, u32[]{:S(2)}, u32[]{:S(2)}) collective-permute-start(bf16[2,128,128]{2,1,0:T(8,128)(2,1)S(1)} %get-tuple-element.32), channel_id=1, source_target_pairs={{0,2},{1,3},{2,4},{3,5},{4,6},{5,7},{6,0},{7,1},{8,10},{9,11},{10,... | collective-permute-start | bytes 196616 | tf_op jit(solution)/shard_map/gather_kv_zh/ppermute | solution.py:320
  53.3 17.3 %collective-permute-start.10 = (bf16[4,2,128,128]{3,2,1,0:T(8,128)(2,1)S(1)}, bf16[4,2,128,128]{3,2,1,0:T(8,128)(2,1)S(1)}, u32[]{:S(2)}, u32[]{:S(2)}) collective-permute-start(bf16[4,2,128,128]{3,2,1,0:T(8,128)(2,1)S(1)} %get-tuple-element.28), channel_id=1, source_target_pairs={{0,16},{1,17},{2,18},{3,19},{4,20},{5,21},{6,22},{7,23},{8,24},{9,... | collective-permute-start | bytes 786440 | tf_op jit(solution)/shard_map/gather_kv_y/ppermute | solution.py:338
  56.5 18.2 %collective-permute-start.9 = (bf16[4,2,128,128]{3,2,1,0:T(8,128)(2,1)S(1)}, bf16[4,2,128,128]{3,2,1,0:T(8,128)(2,1)S(1)}, u32[]{:S(2)}, u32[]{:S(2)}) collective-permute-start(bf16[4,2,128,128]{3,2,1,0:T(8,128)(2,1)S(1)} %get-tuple-element.28), channel_id=1, source_target_pairs={{0,24},{1,25},{2,26},{3,27},{4,28},{5,29},{6,30},{7,31},{8,0},{9,1... | collective-permute-start | bytes 786440 | tf_op jit(solution)/shard_map/gather_kv_y/ppermute | solution.py:338
  58.4 16.3 %collective-permute-start.11 = (bf16[4,2,128,128]{3,2,1,0:T(8,128)(2,1)S(1)}, bf16[4,2,128,128]{3,2,1,0:T(8,128)(2,1)}, u32[]{:S(2)}, u32[]{:S(2)}) collective-permute-start(bf16[4,2,128,128]{3,2,1,0:T(8,128)(2,1)S(1)} %get-tuple-element.28), channel_id=1, source_target_pairs={{0,8},{1,9},{2,10},{3,11},{4,12},{5,13},{6,14},{7,15},{8,16},{9,17... | collective-permute-start | bytes 786440 | tf_op jit(solution)/shard_map/gather_kv_y/ppermute | solution.py:338
  64.1 28.6 %collective-permute-start.5 = (bf16[4192,128]{1,0:T(8,128)(2,1)S(1)}, bf16[4192,128]{1,0:T(8,128)(2,1)}, u32[]{:S(2)}, u32[]{:S(2)}) collective-permute-start(bf16[4192,128]{1,0:T(8,128)(2,1)S(1)} %constant_dynamic-update-slice_fusion.6.pay0), channel_id=1, source_target_pairs={{0,128},{32,160},{64,192},{96,224},{128,256},{160,288},{192,320},{... | collective-permute-start | bytes 3219464 | tf_op jit(solution)/shard_map/gather_q_x/ppermute | solution.py:343
  67.5 30.1 %collective-permute-start.4 = (bf16[4192,128]{1,0:T(8,128)(2,1)S(1)}, bf16[4192,128]{1,0:T(8,128)(2,1)}, u32[]{:S(2)}, u32[]{:S(2)}) collective-permute-start(bf16[4192,128]{1,0:T(8,128)(2,1)S(1)} %constant_dynamic-update-slice_fusion.6.pay0), channel_id=1, source_target_pairs={{0,256},{32,288},{64,320},{96,352},{128,384},{160,416},{192,448},{... | collective-permute-start | bytes 3219464 | tf_op jit(solution)/shard_map/gather_q_x/ppermute | solution.py:343
  70.6 4.1 %copy-start.6 = (bf16[4,2,128,128]{3,2,1,0:T(8,128)(2,1)}, bf16[4,2,128,128]{3,2,1,0:T(8,128)(2,1)S(1)}, u32[]{:S(2)}) copy-start(bf16[4,2,128,128]{3,2,1,0:T(8,128)(2,1)S(1)} %collective-permute-done.10) | copy-start | bytes 786436
  70.6 46.2 %collective-permute-start.3 = (bf16[4192,128]{1,0:T(8,128)(2,1)S(1)}, bf16[4192,128]{1,0:T(8,128)(2,1)}, u32[]{:S(2)}, u32[]{:S(2)}) collective-permute-start(bf16[4192,128]{1,0:T(8,128)(2,1)S(1)} %constant_dynamic-update-slice_fusion.6.pay0), channel_id=1, source_target_pairs={{0,384},{32,416},{64,448},{96,480},{128,0},{160,32},{192,64},{224,... | collective-permute-start | bytes 3219464 | tf_op jit(solution)/shard_map/gather_q_x/ppermute | solution.py:343
  74.7 0.7 copy-start.7
  75.4 3.4 %copy-start.5 = (s32[65536]{0:T(1024)S(1)}, s32[65536]{0:T(1024)}, u32[]{:S(2)}) copy-start(s32[65536]{0:T(1024)} %param.16) | copy-start | bytes 786436
  75.4 41.4 %copy-start = (s32[16,1,1,32]{3,2,1,0:T(1,128)S(1)}, s32[16,1,1,32]{3,2,1,0:T(1,128)}, u32[]{:S(2)}) copy-start(s32[16,1,1,32]{3,2,1,0:T(1,128)} %param.18) | copy-start | bytes 6148
  75.4 41.4 %copy-start.1 = (s32[16,1,1]{0,2,1:T(1,128)S(1)}, s32[16,1,1]{0,2,1:T(1,128)}, u32[]{:S(2)}) copy-start(s32[16,1,1]{0,2,1:T(1,128)} %param.19) | copy-start | bytes 196
  76.7 40.2 %collective-permute-start.12 = (bf16[16,2,128,128]{3,2,1,0:T(8,128)(2,1)S(1)}, bf16[16,2,128,128]{3,2,1,0:T(8,128)(2,1)S(1)}, u32[]{:S(2)}, u32[]{:S(2)}) collective-permute-start(bf16[16,2,128,128]{3,2,1,0:T(8,128)(2,1)S(1)} %bitcast.93), channel_id=1, source_target_pairs={{0,1},{1,0},{2,3},{3,2},{4,5},{5,4},{6,7},{7,6},{8,9},{9,8},{10,11... | collective-permute-start | bytes 3145736 | tf_op jit(solution)/shard_map/gather_kv_core/ppermute | solution.py:341
  141.5 23.4 %copy-start.2 = (bf16[2,16,2,128,128]{4,3,2,1,0:T(8,128)(2,1)S(1)}, bf16[2,16,2,128,128]{4,3,2,1,0:T(8,128)(2,1)}, u32[]{:S(2)}) copy-start(bf16[2,16,2,128,128]{4,3,2,1,0:T(8,128)(2,1)} %get-tuple-element.12) | copy-start | bytes 6291460
  142.9 21.9 %collective-permute-start.19 = (bf16[16,2,128,128]{3,2,1,0:T(8,128)(2,1)S(1)}, bf16[16,2,128,128]{3,2,1,0:T(8,128)(2,1)S(1)}, u32[]{:S(2)}, u32[]{:S(2)}) collective-permute-start(bf16[16,2,128,128]{3,2,1,0:T(8,128)(2,1)S(1)} %slice_bitcast_fusion), channel_id=1, source_target_pairs={{0,1},{1,0},{2,3},{3,2},{4,5},{5,4},{6,7},{7,6},{8,9},{9,8},{10,11... | collective-permute-start | bytes 3145736 | tf_op jit(solution)/shard_map/scatter_kv_core/ppermute | solution.py:351
  145.5 25.7 %collective-permute-start.13 = (bf16[2048,128]{1,0:T(8,128)(2,1)S(1)}, bf16[2048,128]{1,0:T(8,128)(2,1)S(1)}, u32[]{:S(2)}, u32[]{:S(2)}) collective-permute-start(bf16[2048,128]{1,0:T(8,128)(2,1)S(1)} %get-tuple-element.9), channel_id=1, source_target_pairs={{0,128},{32,160},{64,192},{96,224},{128,256},{160,288},{192,320},{... | collective-permute-start | bytes 1572872 | tf_op jit(solution)/shard_map/scatter_q_x/ppermute | solution.py:355
  147.4 33.6 %collective-permute-start.14 = (bf16[2048,128]{1,0:T(8,128)(2,1)S(1)}, bf16[2048,128]{1,0:T(8,128)(2,1)S(1)}, u32[]{:S(2)}, u32[]{:S(2)}) collective-permute-start(bf16[2048,128]{1,0:T(8,128)(2,1)S(1)} %get-tuple-element.10), channel_id=1, source_target_pairs={{0,256},{32,288},{64,320},{96,352},{128,384},{160,416},{192,448},{... | collective-permute-start | bytes 1572872 | tf_op jit(solution)/shard_map/scatter_q_x/ppermute | solution.py:355
  160.9 23.5 %collective-permute-start.15 = (bf16[2048,128]{1,0:T(8,128)(2,1)S(1)}, bf16[2048,128]{1,0:T(8,128)(2,1)S(1)}, u32[]{:S(2)}, u32[]{:S(2)}) collective-permute-start(bf16[2048,128]{1,0:T(8,128)(2,1)S(1)} %get-tuple-element.11), channel_id=1, source_target_pairs={{0,384},{32,416},{64,448},{96,480},{128,0},{160,32},{192,64},{224,... | collective-permute-start | bytes 1572872 | tf_op jit(solution)/shard_map/scatter_q_x/ppermute | solution.py:355
  165.3 26.6 %collective-permute-start.20 = (bf16[4,2,128,128]{3,2,1,0:T(8,128)(2,1)S(1)}, bf16[4,2,128,128]{3,2,1,0:T(8,128)(2,1)S(1)}, u32[]{:S(2)}, u32[]{:S(2)}) collective-permute-start(bf16[4,2,128,128]{3,2,1,0:T(8,128)(2,1)S(1)} %get-tuple-element.18), channel_id=1, source_target_pairs={{0,8},{1,9},{2,10},{3,11},{4,12},{5,13},{6,14},{7,15},{8,16},{9,17... | collective-permute-start | bytes 786440 | tf_op jit(solution)/shard_map/scatter_kv_y/ppermute | solution.py:359
  168.9 43.7 %collective-permute-start.22 = (bf16[4,2,128,128]{3,2,1,0:T(8,128)(2,1)S(1)}, bf16[4,2,128,128]{3,2,1,0:T(8,128)(2,1)S(1)}, u32[]{:S(2)}, u32[]{:S(2)}) collective-permute-start(bf16[4,2,128,128]{3,2,1,0:T(8,128)(2,1)S(1)} %get-tuple-element.19), channel_id=1, source_target_pairs={{0,24},{1,25},{2,26},{3,27},{4,28},{5,29},{6,30},{7,31},{8,0},{9,1... | collective-permute-start | bytes 786440 | tf_op jit(solution)/shard_map/scatter_kv_y/ppermute | solution.py:359
  171.1 41.5 %collective-permute-start.21 = (bf16[4,2,128,128]{3,2,1,0:T(8,128)(2,1)S(1)}, bf16[4,2,128,128]{3,2,1,0:T(8,128)(2,1)S(1)}, u32[]{:S(2)}, u32[]{:S(2)}) collective-permute-start(bf16[4,2,128,128]{3,2,1,0:T(8,128)(2,1)S(1)} %get-tuple-element.20), channel_id=1, source_target_pairs={{0,16},{1,17},{2,18},{3,19},{4,20},{5,21},{6,22},{7,23},{8,24},{9,... | collective-permute-start | bytes 786440 | tf_op jit(solution)/shard_map/scatter_kv_y/ppermute | solution.py:359
  184.7 37.9 %collective-permute-start.16 = (bf16[512,128]{1,0:T(8,128)(2,1)S(1)}, bf16[512,128]{1,0:T(8,128)(2,1)S(1)}, u32[]{:S(2)}, u32[]{:S(2)}) collective-permute-start(bf16[512,128]{1,0:T(8,128)(2,1)S(1)} %get-tuple-element.21), channel_id=1, source_target_pairs={{0,32},{32,64},{64,96},{96,0},{128,160},{160,192},{192,224},{224,1... | collective-permute-start | bytes 393224 | tf_op jit(solution)/shard_map/scatter_q_zl/ppermute | solution.py:363
  186.6 48.4 %collective-permute-start.18 = (bf16[512,128]{1,0:T(8,128)(2,1)S(1)}, bf16[512,128]{1,0:T(8,128)(2,1)S(1)}, u32[]{:S(2)}, u32[]{:S(2)}) collective-permute-start(bf16[512,128]{1,0:T(8,128)(2,1)S(1)} %get-tuple-element.22), channel_id=1, source_target_pairs={{0,96},{32,0},{64,32},{96,64},{128,224},{160,128},{192,160},{224,1... | collective-permute-start | bytes 393224 | tf_op jit(solution)/shard_map/scatter_q_zl/ppermute | solution.py:363
  191.9 43.2 %collective-permute-start.17 = (bf16[512,128]{1,0:T(8,128)(2,1)S(1)}, bf16[512,128]{1,0:T(8,128)(2,1)S(1)}, u32[]{:S(2)}, u32[]{:S(2)}) collective-permute-start(bf16[512,128]{1,0:T(8,128)(2,1)S(1)} %get-tuple-element.23), channel_id=1, source_target_pairs={{0,64},{32,96},{64,0},{96,32},{128,192},{160,224},{192,128},{224,1... | collective-permute-start | bytes 393224 | tf_op jit(solution)/shard_map/scatter_q_zl/ppermute | solution.py:363
  212.8 23.0 %collective-permute-start.23 = (bf16[2,128,128]{2,1,0:T(8,128)(2,1)S(1)}, bf16[2,128,128]{2,1,0:T(8,128)(2,1)S(1)}, u32[]{:S(2)}, u32[]{:S(2)}) collective-permute-start(bf16[2,128,128]{2,1,0:T(8,128)(2,1)S(1)} %get-tuple-element.24), channel_id=1, source_target_pairs={{0,2},{1,3},{2,4},{3,5},{4,6},{5,7},{6,0},{7,1},{8,10},{9,11},{10,... | collective-permute-start | bytes 196616 | tf_op jit(solution)/shard_map/scatter_kv_zh/ppermute | solution.py:367
  215.8 20.0 %collective-permute-start.25 = (bf16[2,128,128]{2,1,0:T(8,128)(2,1)S(1)}, bf16[2,128,128]{2,1,0:T(8,128)(2,1)S(1)}, u32[]{:S(2)}, u32[]{:S(2)}) collective-permute-start(bf16[2,128,128]{2,1,0:T(8,128)(2,1)S(1)} %get-tuple-element.25), channel_id=1, source_target_pairs={{0,6},{1,7},{2,0},{3,1},{4,2},{5,3},{6,4},{7,5},{8,14},{9,15},{10,... | collective-permute-start | bytes 196616 | tf_op jit(solution)/shard_map/scatter_kv_zh/ppermute | solution.py:367
  222.6 20.4 %collective-permute-start.24 = (bf16[2,128,128]{2,1,0:T(8,128)(2,1)S(1)}, bf16[2,128,128]{2,1,0:T(8,128)(2,1)S(1)}, u32[]{:S(2)}, u32[]{:S(2)}) collective-permute-start(bf16[2,128,128]{2,1,0:T(8,128)(2,1)S(1)} %get-tuple-element.26), channel_id=1, source_target_pairs={{0,4},{1,5},{2,6},{3,7},{4,0},{5,1},{6,2},{7,3},{8,12},{9,13},{10,... | collective-permute-start | bytes 196616 | tf_op jit(solution)/shard_map/scatter_kv_zh/ppermute | solution.py:367
where the time goes:
time: 245 us; the launch traced here: 244 us
  starting transfers between devices  144 us (59%)
  waiting for transfers between devices  58.8 us (24%)
  Pallas kernels  24.6 us (10%)
  other arithmetic  11.1 us (5%)
  local copies, waits for them, and re-layouts  3.61 us (1%)
    ppermute x3, waiting for transfers between devices, on_device(): lax.ppermute(wide, 'row', row_perm(-s, 0))  35.2 us
    ppermute x3, starting transfers between devices, on_device(): lax.ppermute(dq[s], 'row', row_perm(0, s))  27.9 us
    pallas_call x1, Pallas kernels, run_attention(): pl.pallas_call(functools.partial(attention_kernel, jcount), out_shape=[pa...  24.6 us
    ppermute x3, starting transfers between devices, on_device(): lax.ppermute(pair, 'col', col_perm(0, -s, 0))  24.6 us
    ppermute x3, starting transfers between devices, on_device(): lax.ppermute(mine[s], 'col', col_perm(0, s, 0))  22.2 us
    ppermute x3, starting transfers between devices, on_device(): lax.ppermute(dqs[s], 'row', row_perm(s, 0))  19.3 us
    ppermute x3, starting transfers between devices, on_device(): lax.ppermute(mine[s], 'col', col_perm(s, 0, 0))  15.8 us
    ppermute x3, waiting for transfers between devices, on_device(): lax.ppermute(pair, 'col', col_perm(0, -s, 0))  13.2 us
  transfers between devices with their start and end apart: 26, of which 7 were waited for; matrix products, arithmetic and copies ran while one was open for 5% of the time, Pallas kernels for 0%

commit v1 on v0

v1 whole, which is shorter than its diff:
```python
import functools
import itertools

import jax
import jax.numpy as jnp
from jax import lax
from jax.experimental import pallas as pl
from jax.experimental.pallas import tpu as pltpu
from jax.sharding import PartitionSpec as P

NX, NZL, NY, NZH, NCORE = 4, 4, 4, 4, 2
SEGMENTS = 11
LOG2E = 1.4426950408889634
ROUND = 4


def flat(x, zl, y, zh, core):
    return (((x * NZL + zl) * NY + y) * NZH + zh) * NCORE + core


def spans(*sizes):
    return itertools.product(*(range(size) for size in sizes))


COLUMNS = [
    [flat(x, zl, y, zh, core) for y in range(NY)]
    for x, zl, zh, core in spans(NX, NZL, NZH, NCORE)
]
DEALS = [
    [flat((x - zh) % NX, (zl - zh) % NZL, y, zh, core) for zh in range(NZH)]
    for x, zl, y, core in spans(NX, NZL, NY, NCORE)
]


def exchange(value, members):
    return lax.all_to_all(value, ("row", "col"), 0, 0, axis_index_groups=members)


def gather(value, members):
    return exchange(jnp.broadcast_to(value, (4,) + value.shape), members)


def shift_x(value, by):
    pairs = [(x * NZL + zl, ((x + by) % NX) * NZL + zl) for x, zl in spans(NX, NZL)]
    return lax.ppermute(value, "row", pairs)


def flip_zl(value, bits):
    return lax.ppermute(value, "row", [(row, row ^ bits) for row in range(NX * NZL)])


def flip_core(value):
    return lax.ppermute(value, "col", [(col, col ^ 1) for col in range(NY * NZH * NCORE)])


def split3(value):
    high = lax.reduce_precision(value, 8, 7)
    rest = value - high
    mid = lax.reduce_precision(rest, 8, 7)
    low = rest - mid
    return [part.astype(jnp.bfloat16) for part in (high, mid, low)]


def segment_table(segment, prefix):
    ids = jnp.arange(SEGMENTS, dtype=jnp.int32)
    start = jnp.sum((segment[None, :] < ids[:, None]).astype(jnp.int32), axis=1)
    finish = jnp.sum((segment[None, :] <= ids[:, None]).astype(jnp.int32), axis=1)
    owner = jnp.max(jnp.where(segment[None, :] == ids[:, None], prefix[None, :], 0), axis=1)
    picked = owner[:, None] == ids[None, :]
    low = jnp.sum(jnp.where(picked, start[None, :], 0), axis=1)
    high = jnp.sum(jnp.where(picked, finish[None, :], 0), axis=1)
    return jnp.stack([start, low, high, finish])


def attention_kernel(jcount, ids_ref, table_ref, *refs):
    f32, bf16 = jnp.float32, jnp.bfloat16
    rows = jcount * 32
    own_ref, second_ref, outer_ref = refs[0:3]
    ahead_near, ahead_far, behind_near, behind_far, opposite_even, opposite_odd = refs[3:9]
    kv0, kv1 = refs[9:11]
    dqs, mine_ref, other_ref = refs[11:15], refs[15], refs[16]
    (
        k_scr,
        v_scr,
        kt_scr,
        dk_scr,
        dv_scr,
        lse_scr,
        delta_scr,
        q_scr,
        do_scr,
        qt_scr,
        dot_scr,
        dqt_scr,
        low_scr,
        pre_low_scr,
        pre_high_scr,
        place_scr,
        full_list,
        part_list,
    ) = refs[17:]
    scale = 128.0 ** -0.5
    my_x, my_zl, my_c = ids_ref[0], ids_ref[1], ids_ref[2]
    deal_x, deal_zl, my_core = ids_ref[3], ids_ref[4], ids_ref[5]

    def source(xs, zs):
        if xs == 2:
            return (opposite_odd if zs & 1 else opposite_even).at[zs >> 1]
        if xs == 0:
            return outer_ref.at[zs >> 1] if zs & 1 else (second_ref if zs else own_ref)
        near, far = (ahead_near, ahead_far) if xs == 1 else (behind_near, behind_far)
        return far.at[{2: 0, 1: 1, 3: 2}[zs]] if zs else near

    dk_scr[...] = jnp.zeros_like(dk_scr)
    dv_scr[...] = jnp.zeros_like(dv_scr)
    dqt_scr[...] = jnp.zeros_like(dqt_scr)

    def prepare(slot, _):
        for half, ref in enumerate((kv0, kv1)):
            at = pl.ds(pl.multiple_of((half ^ my_core) * 128, 128), 128)
            k_scr[slot, at, :] = ref[slot, 0]
            v_scr[slot, at, :] = ref[slot, 1]
        kt_scr[slot] = k_scr[slot].T
        return 0

    lax.fori_loop(0, 16, prepare, 0)

    lane_part = lax.broadcasted_iota(jnp.int32, (4, 128), 1) >> 5
    for xs in range(NX):
        lanes = pl.ds(xs * 128, 128)
        for b in range(4):
            lse = jnp.zeros((4, 128), f32)
            delta = jnp.zeros((4, 128), f32)
            for zs in range(NZL):
                aux = source(xs, zs)[pl.ds(2 * rows, 32), :].astype(f32)
                turn = ((zs - b) * 32) % 128
                here = lane_part == zs
                lse_part = aux[0:4] + aux[4:8] + aux[8:12]
                delta_part = aux[12:16] + aux[16:20] + aux[20:24]
                if turn:
                    lse_part = pltpu.roll(lse_part, turn, 1)
                    delta_part = pltpu.roll(delta_part, turn, 1)
                lse = jnp.where(here, lse_part, lse)
                delta = jnp.where(here, delta_part, delta)
            lse_scr[b, :, lanes] = lse * LOG2E
            delta_scr[b, :, lanes] = delta

    lane = lax.broadcasted_iota(jnp.int32, (jcount, 512), 1)
    row_of = ((my_x + (lane >> 7)) & 3) * 4 + (my_zl ^ ((lane >> 5) & 3))
    block = lax.broadcasted_iota(jnp.int32, (jcount, 512), 0) * 32 + my_c
    place = block * 128 + row_of * 8 + (lane & 7)
    own_low = jnp.zeros_like(place)
    pre_low = jnp.zeros_like(place)
    pre_high = jnp.zeros_like(place)
    for s in range(SEGMENTS):
        here = place >= table_ref[0, s]
        own_low = jnp.where(here, table_ref[0, s], own_low)
        pre_low = jnp.where(here, table_ref[1, s], pre_low)
        pre_high = jnp.where(here, table_ref[2, s], pre_high)
    place_scr[...] = place
    low_scr[...] = own_low
    pre_low_scr[...] = pre_low
    pre_high_scr[...] = jnp.minimum(pre_high, place + 1)
    key_iota = lax.broadcasted_iota(jnp.int32, (256, 512), 0)

    def group_of(zh):
        return ((deal_x - zh) & 3) * 4 + ((deal_zl - zh) & 3)

    def first_of(slot):
        return (group_of(slot & 3) * 16 + slot) * 256

    def sort_block(j, counts):
        base = (j * 32 + my_c) * 128
        first_low, last_low = jnp.int32(0), jnp.int32(0)
        hull_low, hull_high = jnp.int32(1 << 30), jnp.int32(0)
        for s in range(SEGMENTS):
            start, low, high = table_ref[0, s], table_ref[1, s], table_ref[2, s]
            finish = table_ref[3, s]
            first_low = jnp.where(base >= start, start, first_low)
            last_low = jnp.where(base + 127 >= start, start, last_low)
            meets = (start <= base + 127) & (finish > base) & (finish > start)
            hull_low = jnp.where(meets, jnp.minimum(hull_low, low), hull_low)
            hull_high = jnp.where(meets, jnp.maximum(hull_high, high), hull_high)
        hull_high = jnp.minimum(hull_high, base + 128)
        single = first_low == last_low
        tile_high = jnp.where(single, jnp.minimum(hull_high, base + 1), 0)

        def seek(zh, counts):
            def look(y, counts):
                fulls, parts = counts
                slot = y * 4 + zh
                first = first_of(slot)
                active = (first <= base + 127) & (first + 255 >= first_low)
                active = active | ((first < hull_high) & (first + 255 >= hull_low))
                full = (first >= last_low) & (first + 255 <= base)
                full = full | (single & (first >= hull_low) & (first + 256 <= tile_high))
                full_list[fulls] = j * 16 + slot
                part_list[parts] = j * 16 + slot
                return (
                    fulls + jnp.where(active & full, 1, 0),
                    parts + jnp.where(active & jnp.logical_not(full), 1, 0),
                )

            return lax.fori_loop(0, jnp.where(group_of(zh) <= j, 4, 0), look, counts)

        for xs in range(NX):
            for zs in range(NZL):
                at = (xs * NZL + zs) * 32
                ref = source(xs, zs)
                q_scr[j, pl.ds(at, 32), :] = ref[pl.ds(j * 32, 32), :]
                do_scr[j, pl.ds(at, 32), :] = ref[pl.ds(rows + j * 32, 32), :]
        qt_scr[j] = q_scr[j].T
        dot_scr[j] = do_scr[j].T
        return lax.fori_loop(0, 4, seek, counts)

    zero = jnp.int32(0)
    full_count, part_count = lax.fori_loop(0, jcount, sort_block, (zero, zero))

    def work(items, masked):
        items = [(item >> 4, item & 15) for item in items]
        scores = [
            jnp.dot(k_scr[slot], qt_scr[j], preferred_element_type=f32) for j, slot in items
        ]
        weight_grads = [
            jnp.dot(v_scr[slot], dot_scr[j], preferred_element_type=f32) for j, slot in items
        ]
        weights_b, score_grads_b = [], []
        for (j, slot), score, weight_grad in zip(items, scores, weight_grads):
            lse_row = lse_scr[j & 3, pl.ds(j >> 2, 1), :]
            delta_row = delta_scr[j & 3, pl.ds(j >> 2, 1), :]
            weights = jnp.exp2(score * (scale * LOG2E) - lse_row)
            if masked:
                key_at = key_iota + first_of(slot)
                row = pl.ds(j, 1)
                own = (key_at >= low_scr[row, :]) & (key_at <= place_scr[row, :])
                pre = (key_at >= pre_low_scr[row, :]) & (key_at < pre_high_scr[row, :])
                weights = jnp.where(own | pre, weights, 0.0)
            score_grad = weights * (weight_grad - delta_row)
            weights_b.append(weights.astype(bf16))
            score_grads_b.append(score_grad.astype(bf16))
        for (j, slot), weight, score_grad in zip(items, weights_b, score_grads_b):
            dv_scr[slot] += jnp.dot(weight, do_scr[j], preferred_element_type=f32)
            dk_scr[slot] += jnp.dot(score_grad, q_scr[j], preferred_element_type=f32)
            dqt_scr[j] += jnp.dot(kt_scr[slot], score_grad, preferred_element_type=f32)

    def sweep(items, count, masked):
        begin = zero
        for size in (ROUND, 1):
            turns = (count - begin) // size

            def turn(at, _, begin=begin, size=size):
                work([items[begin + at * size + u] for u in range(size)], masked)
                return 0

            lax.fori_loop(0, turns, turn, 0)
            begin = begin + turns * size

    sweep(full_list, full_count, False)
    sweep(part_list, part_count, True)

    def write_queries(j, _):
        dq = (dqt_scr[j] * scale).astype(bf16).T
        for xs in range(NX):
            for zs in range(NZL):
                at = (xs * NZL + zs) * 32
                dqs[xs][pl.ds(zs * rows + j * 32, 32), :] = dq[at : at + 32]
        return 0

    lax.fori_loop(0, jcount, write_queries, 0)

    def finish(slot, _):
        for half, ref in enumerate((mine_ref, other_ref)):
            at = pl.ds(pl.multiple_of((half ^ my_core) * 128, 128), 128)
            ref[slot, 0] = (dk_scr[slot, at, :] * scale).astype(bf16)
            ref[slot, 1] = dv_scr[slot, at, :].astype(bf16)
        return 0

    lax.fori_loop(0, 16, finish, 0)


def run_attention(ids, table, payloads, kv0, kv1, jcount):
    f32, bf16 = jnp.float32, jnp.bfloat16
    rows = jcount * 32
    smem = pl.BlockSpec(memory_space=pltpu.SMEM)
    vmem = pl.BlockSpec(memory_space=pltpu.VMEM)
    part = jax.ShapeDtypeStruct((NZL * rows, 128), bf16)
    return pl.pallas_call(
        functools.partial(attention_kernel, jcount),
        out_shape=[part] * 4 + [jax.ShapeDtypeStruct((16, 2, 128, 128), bf16)] * 2,
        in_specs=[smem] * 2 + [vmem] * 11,
        out_specs=[vmem] * 6,
        scratch_shapes=[
            pltpu.VMEM((16, 256, 128), bf16),
            pltpu.VMEM((16, 256, 128), bf16),
            pltpu.VMEM((16, 128, 256), bf16),
            pltpu.VMEM((16, 256, 128), f32),
            pltpu.VMEM((16, 256, 128), f32),
            pltpu.VMEM((4, 4, 512), f32),
            pltpu.VMEM((4, 4, 512), f32),
            pltpu.VMEM((jcount, 512, 128), bf16),
            pltpu.VMEM((jcount, 512, 128), bf16),
            pltpu.VMEM((jcount, 128, 512), bf16),
            pltpu.VMEM((jcount, 128, 512), bf16),
            pltpu.VMEM((jcount, 128, 512), f32),
            pltpu.VMEM((jcount, 512), jnp.int32),
            pltpu.VMEM((jcount, 512), jnp.int32),
            pltpu.VMEM((jcount, 512), jnp.int32),
            pltpu.VMEM((jcount, 512), jnp.int32),
            pltpu.SMEM((jcount * 16 + 1,), jnp.int32),
            pltpu.SMEM((jcount * 16 + 1,), jnp.int32),
        ],
        compiler_params=pltpu.CompilerParams(vmem_limit_bytes=48 * 1024 * 1024),
        name="attention_backward",
    )(ids, table, *payloads, kv0, kv1)


def total(parts):
    out = parts[0].astype(jnp.float32)
    for part in parts[1:]:
        out = out + part.astype(jnp.float32)
    return out.astype(jnp.bfloat16)


def on_device(
    queries,
    grad_output,
    attn_output,
    key_states,
    value_states,
    log_sum,
    segment,
    prefix,
    block_list,
    block_count,
):
    jcount = queries.shape[0]
    rows = jcount * 32
    row = lax.axis_index("row")
    col = lax.axis_index("col")
    my_x, my_zl, my_zh = row // NZL, row % NZL, (col // NCORE) % NZH
    ids = jnp.stack([my_x, my_zl, col, my_x + my_zh, my_zl + my_zh, col % NCORE])
    ids = ids.astype(jnp.int32)

    def heads_first(value):
        return value.reshape(jcount, 8, 4, 128).transpose(0, 2, 1, 3).reshape(rows, 128)

    with jax.named_scope("pack"):
        delta = jnp.sum(
            (grad_output.astype(jnp.float32) * attn_output.astype(jnp.float32)).reshape(
                jcount, 8, 4, 128
            ),
            axis=3,
        )
        lse = log_sum.reshape(jcount, 8, 4)
        aux = jnp.stack(
            split3(lse.transpose(0, 2, 1).reshape(jcount, 32))
            + split3(delta.transpose(0, 2, 1).reshape(jcount, 32))
        )
        payload = jnp.concatenate(
            [
                heads_first(queries),
                heads_first(grad_output),
                aux.reshape(-1, 128),
                jnp.zeros((8, 128), jnp.bfloat16),
            ],
            axis=0,
        )
        pair = jnp.stack([key_states, value_states])

    with jax.named_scope("gather_q_zl"):
        second = flip_zl(payload, 2)
        outer = flip_zl(jnp.stack([payload, second]), 1)
        others = jnp.concatenate([second[None], outer], axis=0)
    with jax.named_scope("gather_q_near"):
        near = [shift_x(payload, -1), shift_x(payload, 1)]
    with jax.named_scope("gather_kv_deal"):
        kv = gather(pair, DEALS)
    with jax.named_scope("gather_q_far"):
        others, *near = lax.optimization_barrier((others, *near))
        far = [shift_x(others, -1), shift_x(others, 1)]
    with jax.named_scope("gather_kv_y"):
        kv = gather(kv, COLUMNS).reshape(NY * NZH, 2, 128, 128)
    with jax.named_scope("gather_q_relay"):
        even = shift_x(jnp.stack([near[0], far[0][0]]), -1)
        odd = shift_x(far[1][1:], 1)
    with jax.named_scope("gather_kv_core"):
        kv_other = flip_core(kv)

    table = segment_table(segment, prefix)
    payloads = [payload, second, outer, near[0], far[0], near[1], far[1], even, odd]
    *dqs, mine, other = run_attention(ids, table, payloads, kv, kv_other, jcount)

    with jax.named_scope("scatter_kv_core"):
        mine = total([mine, flip_core(other)]).reshape(NY, NZH, 2, 128, 128)
    with jax.named_scope("scatter_q_relay"):
        even = shift_x(dqs[2][: 2 * rows], 1)
        odd = shift_x(dqs[2][2 * rows :], -1)
    with jax.named_scope("scatter_kv_y"):
        mine = total(exchange(mine, COLUMNS))
    with jax.named_scope("scatter_q_x"):
        ahead = total([dqs[1], jnp.concatenate([even, jnp.zeros_like(even)])])
        behind = total([dqs[3], jnp.concatenate([jnp.zeros_like(odd), odd])])
        dq = total([dqs[0], shift_x(ahead, 1), shift_x(behind, -1)])
    with jax.named_scope("scatter_kv_deal"):
        mine = total(exchange(mine, DEALS))
    with jax.named_scope("scatter_q_zl"):
        dq = dq.reshape(NZL, rows, 128)
        dq = total([dq[0::2], flip_zl(dq[1::2], 1)])
        dq = total([dq[0], flip_zl(dq[1], 2)])
    dq = dq.reshape(jcount, 4, 8, 128).transpose(0, 2, 1, 3).reshape(jcount, 1, 8, 512)
    return dq, mine[0], mine[1]


def solution(mesh):
    in_specs = (
        P(None, "col", "row", None),
        P(None, "col", "row", None),
        P(None, "col", "row", None),
        P(("row", "col"), None),
        P(("row", "col"), None),
        P(None, "col", "row", None),
        P(),
        P(),
        P(None, "col", "row", None),
        P(None, "col", "row"),
    )
    out_specs = (P(None, "col", "row", None), P(("row", "col"), None), P(("row", "col"), None))
    return jax.shard_map(
        on_device, mesh=mesh, in_specs=in_specs, out_specs=out_specs, check_vma=False
    )
```

time: 245 us -> 203 us (0.83)
  the two profiles are of different devices: /device:TPU:58 before, /device:TPU:2 now
where the time goes in v1:
time: 203 us; the launch traced here: 206 us
  starting transfers between devices  102 us (50%)
  waiting for transfers between devices  52.6 us (26%)
  Pallas kernels  33.7 us (17%)
  other arithmetic  12.4 us (6%)
  local copies, waits for them, and re-layouts  4.21 us (2%)
    all_to_all x4, starting transfers between devices, exchange(): lax.all_to_all(value, ('row', 'col'), 0, 0, axis_index_groups=members)  42 us
    ppermute x10, starting transfers between devices, shift_x(): return lax.ppermute(value, 'row', pairs)  33.9 us
    pallas_call x1, Pallas kernels, run_attention(): pl.pallas_call(functools.partial(attention_kernel, jcount), out_shape=[pa...  33.7 us
    ppermute x4, starting transfers between devices, flip_zl(): lax.ppermute(value, 'row', [(row, row ^ bits) for row in range(NX * NZL)])  22.3 us
    ppermute x10, waiting for transfers between devices, shift_x(): return lax.ppermute(value, 'row', pairs)  21.8 us
    all_to_all x4, waiting for transfers between devices, exchange(): lax.all_to_all(value, ('row', 'col'), 0, 0, axis_index_groups=members)  20 us
    ppermute x4, waiting for transfers between devices, flip_zl(): lax.ppermute(value, 'row', [(row, row ^ bits) for row in range(NX * NZL)])  10.8 us
  transfers between devices with their start and end apart: 20, of which 10 were waited for; matrix products, arithmetic and copies ran while one was open for 5% of the time, Pallas kernels for 0%

profile of v1, /device:TPU:2, one launch (start us, length us, event | category | flops | bytes accessed | tf_op | source)
XLA Modules:
  0.0 206.0 jit_solution(10600737302764661298)
XLA Ops:
  0.7 1.1 bitcast_reduce_fusion
  1.8 0.1 copy.17
  1.9 0.7 constant_dynamic-update-slice_fusion.5
  2.6 0.7 constant_dynamic-update-slice_fusion.4
  3.3 0.7 constant_dynamic-update-slice_fusion.3
  4.1 0.1 copy.18
  4.2 0.1 reshape.173
  4.3 0.1 pad.13.clone
  4.4 1.2 maximum_maximum_fusion.refs_0_
  5.5 5.2 %collective-permute-start = (bf16[1056,128]{1,0:T(8,128)(2,1)S(1)}, bf16[1056,128]{1,0:T(8,128)(2,1)S(1)}, u32[]{:S(2)}, u32[]{:S(2)}) collective-permute-start(bf16[1056,128]{1,0:T(8,128)(2,1)S(1)} %maximum_maximum_fusion.refs_0_), channel_id=1, source_target_pairs={{0,64},{32,96},{64,0},{96,32},{128,192},{160,224},{192,128},{224,1... | collective-permute-start | bytes 811016 | tf_op jit(solution)/shard_map/gather_q_zl/ppermute | solution.py:49
  10.8 0.7 broadcast_in_dim.60
  11.5 13.9 %all-to-all-start = ((bf16[4,2,128,128]{3,2,1,0:T(8,128)(2,1)}), bf16[4,2,128,128]{3,2,1,0:T(8,128)(2,1)S(1)}, u32[]{:S(2)}, u32[]{:S(2)}) async-start(bf16[4,2,128,128]{3,2,1,0:T(8,128)(2,1)} %broadcast_in_dim.60), calls=%async_computation | async-start | bytes 524288 | tf_op jit(solution)/shard_map/gather_kv_deal/all_to_all | solution.py:36
  25.4 0.0 collective-permute-done.refs_1_
  25.4 0.1 pad_maximum_fusion.1
  25.5 2.9 %collective-permute-start.1 = (bf16[2,1056,128]{2,1,0:T(8,128)(2,1)S(1)}, bf16[2,1056,128]{2,1,0:T(8,128)(2,1)S(1)}, u32[]{:S(2)}, u32[]{:S(2)}) collective-permute-start(bf16[2,1056,128]{2,1,0:T(8,128)(2,1)S(1)} %pad_maximum_fusion.1), channel_id=1, source_target_pairs={{0,32},{32,0},{64,96},{96,64},{128,160},{160,128},{192,224},{224,1... | collective-permute-start | bytes 1622024 | tf_op jit(solution)/shard_map/gather_q_zl/ppermute | solution.py:49
  28.4 1.9 collective-permute-start.3
  30.3 3.9 %collective-permute-start.2 = (bf16[1056,128]{1,0:T(8,128)(2,1)S(1)}, bf16[1056,128]{1,0:T(8,128)(2,1)S(1)}, u32[]{:S(2)}, u32[]{:S(2)}) collective-permute-start(bf16[1056,128]{1,0:T(8,128)(2,1)S(1)} %maximum_maximum_fusion.refs_0_), channel_id=1, source_target_pairs={{0,384},{32,416},{64,448},{96,480},{128,0},{160,32},{192,64},{224,... | collective-permute-start | bytes 811016 | tf_op jit(solution)/shard_map/gather_q_near/ppermute | solution.py:45
  34.3 9.9 %all-to-all-done = bf16[4,2,128,128]{3,2,1,0:T(8,128)(2,1)S(1)} async-done(((bf16[4,2,128,128]{3,2,1,0:T(8,128)(2,1)}), bf16[4,2,128,128]{3,2,1,0:T(8,128)(2,1)S(1)}, u32[]{:S(2)}, u32[]{:S(2)}) %all-to-all-start) | async-done | bytes 262176 | tf_op jit(solution)/shard_map/gather_kv_deal/all_to_all | solution.py:36
  44.2 1.2 broadcast_in_dim.61
  45.4 4.5 %all-to-all-start.1 = ((bf16[4,4,2,128,128]{4,3,2,1,0:T(8,128)(2,1)}), bf16[4,4,2,128,128]{4,3,2,1,0:T(8,128)(2,1)}, u32[]{:S(2)}, u32[]{:S(2)}) async-start(bf16[4,4,2,128,128]{4,3,2,1,0:T(8,128)(2,1)} %broadcast_in_dim.61), calls=%async_computation.1 | async-start | bytes 2097152 | tf_op jit(solution)/shard_map/gather_kv_y/all_to_all | solution.py:36
  49.9 0.0 collective-permute-done.1.refs_2_
  49.9 1.0 pad_maximum_fusion
  50.9 0.0 collective-permute-done.2.refs_3_
  50.9 2.9 %collective-permute-start.5 = (bf16[3,1056,128]{2,1,0:T(8,128)(2,1)}, bf16[3,1056,128]{2,1,0:T(8,128)(2,1)}, u32[]{:S(2)}, u32[]{:S(2)}) collective-permute-start(bf16[3,1056,128]{2,1,0:T(8,128)(2,1)} %pad_maximum_fusion), channel_id=1, source_target_pairs={{0,128},{32,160},{64,192},{96,224},{128,256},{160,288},{192,320},{... | collective-permute-start | bytes 2433032 | tf_op jit(solution)/shard_map/gather_q_far/ppermute | solution.py:45
  53.8 3.4 %collective-permute-start.4 = (bf16[3,1056,128]{2,1,0:T(8,128)(2,1)}, bf16[3,1056,128]{2,1,0:T(8,128)(2,1)S(1)}, u32[]{:S(2)}, u32[]{:S(2)}) collective-permute-start(bf16[3,1056,128]{2,1,0:T(8,128)(2,1)} %pad_maximum_fusion), channel_id=1, source_target_pairs={{0,384},{32,416},{64,448},{96,480},{128,0},{160,32},{192,64},{224,... | collective-permute-start | bytes 2433032 | tf_op jit(solution)/shard_map/gather_q_far/ppermute | solution.py:45
  57.2 6.4 %all-to-all-done.1 = bf16[4,4,2,128,128]{4,3,2,1,0:T(8,128)(2,1)} async-done(((bf16[4,4,2,128,128]{4,3,2,1,0:T(8,128)(2,1)}), bf16[4,4,2,128,128]{4,3,2,1,0:T(8,128)(2,1)}, u32[]{:S(2)}, u32[]{:S(2)}) %all-to-all-start.1) | async-done | bytes 1048608 | tf_op jit(solution)/shard_map/gather_kv_y/all_to_all | solution.py:36
  63.6 1.9 collective-permute-start.8
  65.5 0.1 stack.73.ids_ref
  65.6 5.5 %collective-permute-done.5.refs_6_ = bf16[3,1056,128]{2,1,0:T(8,128)(2,1)} collective-permute-done((bf16[3,1056,128]{2,1,0:T(8,128)(2,1)}, bf16[3,1056,128]{2,1,0:T(8,128)(2,1)}, u32[]{:S(2)}, u32[]{:S(2)}) %collective-permute-start.5) | collective-permute-done | bytes 811040 | tf_op jit(solution)/shard_map/gather_q_far/ppermute | solution.py:45
  71.1 1.1 slice.59
  72.2 0.0 copy-start.1
  72.2 0.0 copy-start.2
  72.2 2.9 %collective-permute-start.7 = (bf16[2,1056,128]{2,1,0:T(8,128)(2,1)S(1)}, bf16[2,1056,128]{2,1,0:T(8,128)(2,1)S(1)}, u32[]{:S(2)}, u32[]{:S(2)}) collective-permute-start(bf16[2,1056,128]{2,1,0:T(8,128)(2,1)S(1)} %slice.59), channel_id=1, source_target_pairs={{0,128},{32,160},{64,192},{96,224},{128,256},{160,288},{192,320},{... | collective-permute-start | bytes 1622024 | tf_op jit(solution)/shard_map/gather_q_relay/ppermute | solution.py:45
  75.2 0.1 pad_maximum_fusion.2
  75.3 3.4 %collective-permute-start.6 = (bf16[2,1056,128]{2,1,0:T(8,128)(2,1)S(1)}, bf16[2,1056,128]{2,1,0:T(8,128)(2,1)S(1)}, u32[]{:S(2)}, u32[]{:S(2)}) collective-permute-start(bf16[2,1056,128]{2,1,0:T(8,128)(2,1)S(1)} %pad_maximum_fusion.2), channel_id=1, source_target_pairs={{0,384},{32,416},{64,448},{96,480},{128,0},{160,32},{192,64},{224,... | collective-permute-start | bytes 1622024 | tf_op jit(solution)/shard_map/gather_q_relay/ppermute | solution.py:45
  78.7 2.2 %convert_reduce_fusion.1 = (s32[11]{0:T(128)S(1)}, s32[11]{0:T(128)S(1)}, s32[11]{0:T(128)S(1)}) fusion(s32[65536]{0:T(1024)S(1)} %copy-done.1, s32[65536]{0:T(1024)S(1)} %copy-done.2), kind=kLoop, calls=%fused_computation.4 | loop fusion | flops 6488031 | bytes 524420 | tf_op jit(solution)/shard_map/reduce_sum | solution.py:66
  80.9 0.2 select_reduce_fusion.2
  81.2 4.0 %collective-permute-done.7.refs_8_ = bf16[2,1056,128]{2,1,0:T(8,128)(2,1)S(1)} collective-permute-done((bf16[2,1056,128]{2,1,0:T(8,128)(2,1)S(1)}, bf16[2,1056,128]{2,1,0:T(8,128)(2,1)S(1)}, u32[]{:S(2)}, u32[]{:S(2)}) %collective-permute-start.7) | collective-permute-done | bytes 540704 | tf_op jit(solution)/shard_map/gather_q_relay/ppermute | solution.py:45
  85.1 3.0 %collective-permute-done.6.refs_7_ = bf16[2,1056,128]{2,1,0:T(8,128)(2,1)S(1)} collective-permute-done((bf16[2,1056,128]{2,1,0:T(8,128)(2,1)S(1)}, bf16[2,1056,128]{2,1,0:T(8,128)(2,1)S(1)}, u32[]{:S(2)}, u32[]{:S(2)}) %collective-permute-start.6) | collective-permute-done | bytes 540704 | tf_op jit(solution)/shard_map/gather_q_relay/ppermute | solution.py:45
  88.1 0.0 collective-permute-done.8.refs_10_
  88.1 33.7 %attention_backward.1 = (bf16[2048,128]{1,0:T(8,128)(2,1)S(1)}, bf16[2048,128]{1,0:T(8,128)(2,1)S(1)}, bf16[2048,128]{1,0:T(8,128)(2,1)S(1)}, bf16[2048,128]{1,0...) custom-call(s32[6]{0:T(128)S(1)} %stack.73.ids_ref, ...), custom_call_target="tpu_custom_call" | custom-call | tf_op jit(solution)/shard_map/attention_backward/pallas_call | solution.py:287
  121.8 2.1 collective-permute-start.11
  123.9 1.9 collective-permute-start.15
  125.8 7.7 %collective-permute-start.9 = (bf16[1024,128]{1,0:T(8,128)(2,1)S(1)}, bf16[1024,128]{1,0:T(8,128)(2,1)S(1)}, u32[]{:S(2)}, u32[]{:S(2)}) collective-permute-start(bf16[1024,128]{1,0:T(8,128)(2,1)S(1)} %get-tuple-element.26), channel_id=1, source_target_pairs={{0,128},{32,160},{64,192},{96,224},{128,256},{160,288},{192,320},{... | collective-permute-start | bytes 786440 | tf_op jit(solution)/shard_map/scatter_q_relay/ppermute | solution.py:45
  133.6 0.5 collective-permute-done.11
  134.0 0.1 add_convert_fusion.2
  134.1 2.1 collective-permute-start.12
  136.2 4.4 %collective-permute-done.9 = bf16[1024,128]{1,0:T(8,128)(2,1)S(1)} collective-permute-done((bf16[1024,128]{1,0:T(8,128)(2,1)S(1)}, bf16[1024,128]{1,0:T(8,128)(2,1)S(1)}, u32[]{:S(2)}, u32[]{:S(2)}) %collective-permute-start.9) | collective-permute-done | bytes 262176 | tf_op jit(solution)/shard_map/scatter_q_relay/ppermute | solution.py:45
  140.6 0.1 add_convert_fusion.3
  140.6 3.6 %collective-permute-start.10 = (bf16[2048,128]{1,0:T(8,128)(2,1)S(1)}, bf16[2048,128]{1,0:T(8,128)(2,1)}, u32[]{:S(2)}, u32[]{:S(2)}) collective-permute-start(bf16[2048,128]{1,0:T(8,128)(2,1)S(1)} %add_convert_fusion.3), channel_id=1, source_target_pairs={{0,128},{32,160},{64,192},{96,224},{128,256},{160,288},{192,320},{... | collective-permute-start | bytes 1572872 | tf_op jit(solution)/shard_map/scatter_q_x/ppermute | solution.py:45
  144.2 0.0 collective-permute-done.15
  144.3 1.4 add_convert_fusion
  145.6 7.3 %all-to-all-start.2 = ((bf16[4,4,2,128,128]{4,3,2,1,0:T(8,128)(2,1)}), bf16[4,4,2,128,128]{4,3,2,1,0:T(8,128)(2,1)S(1)}, u32[]{:S(2)}, u32[]{:S(2)}) async-start(bf16[4,4,2,128,128]{4,3,2,1,0:T(8,128)(2,1)} %bitcast.34), calls=%async_computation.2 | async-start | bytes 2097152 | tf_op jit(solution)/shard_map/scatter_kv_y/all_to_all | solution.py:36
  152.9 4.5 %collective-permute-done.10 = bf16[2048,128]{1,0:T(8,128)(2,1)} collective-permute-done((bf16[2048,128]{1,0:T(8,128)(2,1)S(1)}, bf16[2048,128]{1,0:T(8,128)(2,1)}, u32[]{:S(2)}, u32[]{:S(2)}) %collective-permute-start.10) | collective-permute-done | bytes 524320 | tf_op jit(solution)/shard_map/scatter_q_x/ppermute | solution.py:45
  157.4 1.2 add_convert_fusion.1
  158.7 9.7 %collective-permute-start.13 = (bf16[2,512,128]{2,1,0:T(8,128)(2,1)S(1)}, bf16[2,512,128]{2,1,0:T(8,128)(2,1)S(1)}, u32[]{:S(2)}, u32[]{:S(2)}) collective-permute-start(bf16[2,512,128]{2,1,0:T(8,128)(2,1)S(1)} %slice.51), channel_id=1, source_target_pairs={{0,32},{32,0},{64,96},{96,64},{128,160},{160,128},{192,224},{224,1... | collective-permute-start | bytes 786440 | tf_op jit(solution)/shard_map/scatter_q_zl/ppermute | solution.py:49
  168.4 0.8 fusion
  169.3 16.3 %all-to-all-start.3 = ((bf16[4,2,128,128]{3,2,1,0:T(8,128)(2,1)}), bf16[4,2,128,128]{3,2,1,0:T(8,128)(2,1)S(1)}, u32[]{:S(2)}, u32[]{:S(2)}) async-start(bf16[4,2,128,128]{3,2,1,0:T(8,128)(2,1)} %fusion), calls=%async_computation.3 | async-start | bytes 524288 | tf_op jit(solution)/shard_map/scatter_kv_deal/all_to_all | solution.py:36
  185.5 0.1 add_convert_fusion.5
  185.6 4.5 %collective-permute-start.14 = (bf16[512,128]{1,0:T(8,128)(2,1)S(1)}, bf16[512,128]{1,0:T(8,128)(2,1)S(1)}, u32[]{:S(2)}, u32[]{:S(2)}) collective-permute-start(bf16[512,128]{1,0:T(8,128)(2,1)S(1)} %slice_bitcast_fusion), channel_id=1, source_target_pairs={{0,64},{32,96},{64,0},{96,32},{128,192},{160,224},{192,128},{224,1... | collective-permute-start | bytes 393224 | tf_op jit(solution)/shard_map/scatter_q_zl/ppermute | solution.py:49
  190.1 10.8 %collective-permute-done.14 = bf16[512,128]{1,0:T(8,128)(2,1)S(1)} collective-permute-done((bf16[512,128]{1,0:T(8,128)(2,1)S(1)}, bf16[512,128]{1,0:T(8,128)(2,1)S(1)}, u32[]{:S(2)}, u32[]{:S(2)}) %collective-permute-start.14) | collective-permute-done | bytes 131104 | tf_op jit(solution)/shard_map/scatter_q_zl/ppermute | solution.py:49
  200.9 0.7 fusion.1
  201.6 3.7 %all-to-all-done.3 = bf16[4,2,128,128]{3,2,1,0:T(8,128)(2,1)S(1)} async-done(((bf16[4,2,128,128]{3,2,1,0:T(8,128)(2,1)}), bf16[4,2,128,128]{3,2,1,0:T(8,128)(2,1)S(1)}, u32[]{:S(2)}, u32[]{:S(2)}) %all-to-all-start.3) | async-done | bytes 262176 | tf_op jit(solution)/shard_map/scatter_kv_deal/all_to_all | solution.py:36
  205.4 0.6 slice_bitcast_fusion.2
  (26 shorter events, 0.2 us)
Async XLA Ops:
  0.6 10.1 %copy-start.3 = (bf16[128,128]{1,0:T(8,128)(2,1)S(1)}, bf16[128,128]{1,0:T(8,128)(2,1)}, u32[]{:S(2)}) copy-start(bf16[128,128]{1,0:T(8,128)(2,1)} %param.14) | copy-start | bytes 98308
  0.6 10.1 %copy-start.4 = (bf16[128,128]{1,0:T(8,128)(2,1)S(1)}, bf16[128,128]{1,0:T(8,128)(2,1)}, u32[]{:S(2)}) copy-start(bf16[128,128]{1,0:T(8,128)(2,1)} %param.13) | copy-start | bytes 98308
  5.5 19.9 %collective-permute-start = (bf16[1056,128]{1,0:T(8,128)(2,1)S(1)}, bf16[1056,128]{1,0:T(8,128)(2,1)S(1)}, u32[]{:S(2)}, u32[]{:S(2)}) collective-permute-start(bf16[1056,128]{1,0:T(8,128)(2,1)S(1)} %maximum_maximum_fusion.refs_0_), channel_id=1, source_target_pairs={{0,64},{32,96},{64,0},{96,32},{128,192},{160,224},{192,128},{224,1... | collective-permute-start | bytes 811016 | tf_op jit(solution)/shard_map/gather_q_zl/ppermute | solution.py:49
  11.5 32.7 %all-to-all-start = ((bf16[4,2,128,128]{3,2,1,0:T(8,128)(2,1)}), bf16[4,2,128,128]{3,2,1,0:T(8,128)(2,1)S(1)}, u32[]{:S(2)}, u32[]{:S(2)}) async-start(bf16[4,2,128,128]{3,2,1,0:T(8,128)(2,1)} %broadcast_in_dim.60), calls=%async_computation | async-start | bytes 524288 | tf_op jit(solution)/shard_map/gather_kv_deal/all_to_all | solution.py:36
  25.5 24.4 %collective-permute-start.1 = (bf16[2,1056,128]{2,1,0:T(8,128)(2,1)S(1)}, bf16[2,1056,128]{2,1,0:T(8,128)(2,1)S(1)}, u32[]{:S(2)}, u32[]{:S(2)}) collective-permute-start(bf16[2,1056,128]{2,1,0:T(8,128)(2,1)S(1)} %pad_maximum_fusion.1), channel_id=1, source_target_pairs={{0,32},{32,0},{64,96},{96,64},{128,160},{160,128},{192,224},{224,1... | collective-permute-start | bytes 1622024 | tf_op jit(solution)/shard_map/gather_q_zl/ppermute | solution.py:49
  28.4 22.5 %collective-permute-start.3 = (bf16[1056,128]{1,0:T(8,128)(2,1)S(1)}, bf16[1056,128]{1,0:T(8,128)(2,1)S(1)}, u32[]{:S(2)}, u32[]{:S(2)}) collective-permute-start(bf16[1056,128]{1,0:T(8,128)(2,1)S(1)} %maximum_maximum_fusion.refs_0_), channel_id=1, source_target_pairs={{0,128},{32,160},{64,192},{96,224},{128,256},{160,288},{192,320},{... | collective-permute-start | bytes 811016 | tf_op jit(solution)/shard_map/gather_q_near/ppermute | solution.py:45
  30.3 20.6 %collective-permute-start.2 = (bf16[1056,128]{1,0:T(8,128)(2,1)S(1)}, bf16[1056,128]{1,0:T(8,128)(2,1)S(1)}, u32[]{:S(2)}, u32[]{:S(2)}) collective-permute-start(bf16[1056,128]{1,0:T(8,128)(2,1)S(1)} %maximum_maximum_fusion.refs_0_), channel_id=1, source_target_pairs={{0,384},{32,416},{64,448},{96,480},{128,0},{160,32},{192,64},{224,... | collective-permute-start | bytes 811016 | tf_op jit(solution)/shard_map/gather_q_near/ppermute | solution.py:45
  45.4 18.1 %all-to-all-start.1 = ((bf16[4,4,2,128,128]{4,3,2,1,0:T(8,128)(2,1)}), bf16[4,4,2,128,128]{4,3,2,1,0:T(8,128)(2,1)}, u32[]{:S(2)}, u32[]{:S(2)}) async-start(bf16[4,4,2,128,128]{4,3,2,1,0:T(8,128)(2,1)} %broadcast_in_dim.61), calls=%async_computation.1 | async-start | bytes 2097152 | tf_op jit(solution)/shard_map/gather_kv_y/all_to_all | solution.py:36
  50.9 20.2 %collective-permute-start.5 = (bf16[3,1056,128]{2,1,0:T(8,128)(2,1)}, bf16[3,1056,128]{2,1,0:T(8,128)(2,1)}, u32[]{:S(2)}, u32[]{:S(2)}) collective-permute-start(bf16[3,1056,128]{2,1,0:T(8,128)(2,1)} %pad_maximum_fusion), channel_id=1, source_target_pairs={{0,128},{32,160},{64,192},{96,224},{128,256},{160,288},{192,320},{... | collective-permute-start | bytes 2433032 | tf_op jit(solution)/shard_map/gather_q_far/ppermute | solution.py:45
  53.8 21.4 %collective-permute-start.4 = (bf16[3,1056,128]{2,1,0:T(8,128)(2,1)}, bf16[3,1056,128]{2,1,0:T(8,128)(2,1)S(1)}, u32[]{:S(2)}, u32[]{:S(2)}) collective-permute-start(bf16[3,1056,128]{2,1,0:T(8,128)(2,1)} %pad_maximum_fusion), channel_id=1, source_target_pairs={{0,384},{32,416},{64,448},{96,480},{128,0},{160,32},{192,64},{224,... | collective-permute-start | bytes 2433032 | tf_op jit(solution)/shard_map/gather_q_far/ppermute | solution.py:45
  63.6 24.6 %collective-permute-start.8 = (bf16[16,2,128,128]{3,2,1,0:T(8,128)(2,1)}, bf16[16,2,128,128]{3,2,1,0:T(8,128)(2,1)}, u32[]{:S(2)}, u32[]{:S(2)}) collective-permute-start(bf16[16,2,128,128]{3,2,1,0:T(8,128)(2,1)} %bitcast.27.refs_9_), channel_id=1, source_target_pairs={{0,1},{1,0},{2,3},{3,2},{4,5},{5,4},{6,7},{7,6},{8,9},{9,8},{10,11... | collective-permute-start | bytes 3145736 | tf_op jit(solution)/shard_map/gather_kv_core/ppermute | solution.py:53
  72.2 6.5 %copy-start.1 = (s32[65536]{0:T(1024)S(1)}, s32[65536]{0:T(1024)}, u32[]{:S(2)}) copy-start(s32[65536]{0:T(1024)} %param.16) | copy-start | bytes 786436
  72.2 6.5 %copy-start.2 = (s32[65536]{0:T(1024)S(1)}, s32[65536]{0:T(1024)}, u32[]{:S(2)}) copy-start(s32[65536]{0:T(1024)} %param.17) | copy-start | bytes 786436
  72.2 12.9 %collective-permute-start.7 = (bf16[2,1056,128]{2,1,0:T(8,128)(2,1)S(1)}, bf16[2,1056,128]{2,1,0:T(8,128)(2,1)S(1)}, u32[]{:S(2)}, u32[]{:S(2)}) collective-permute-start(bf16[2,1056,128]{2,1,0:T(8,128)(2,1)S(1)} %slice.59), channel_id=1, source_target_pairs={{0,128},{32,160},{64,192},{96,224},{128,256},{160,288},{192,320},{... | collective-permute-start | bytes 1622024 | tf_op jit(solution)/shard_map/gather_q_relay/ppermute | solution.py:45
  75.3 12.8 %collective-permute-start.6 = (bf16[2,1056,128]{2,1,0:T(8,128)(2,1)S(1)}, bf16[2,1056,128]{2,1,0:T(8,128)(2,1)S(1)}, u32[]{:S(2)}, u32[]{:S(2)}) collective-permute-start(bf16[2,1056,128]{2,1,0:T(8,128)(2,1)S(1)} %pad_maximum_fusion.2), channel_id=1, source_target_pairs={{0,384},{32,416},{64,448},{96,480},{128,0},{160,32},{192,64},{224,... | collective-permute-start | bytes 1622024 | tf_op jit(solution)/shard_map/gather_q_relay/ppermute | solution.py:45
  121.8 2.1 %copy-start.5 = (bf16[16,2,128,128]{3,2,1,0:T(8,128)(2,1)S(1)}, bf16[16,2,128,128]{3,2,1,0:T(8,128)(2,1)}, u32[]{:S(2)}) copy-start(bf16[16,2,128,128]{3,2,1,0:T(8,128)(2,1)} %get-tuple-element.20) | copy-start | bytes 3145732
  121.8 12.2 %collective-permute-start.11 = (bf16[1024,128]{1,0:T(8,128)(2,1)S(1)}, bf16[1024,128]{1,0:T(8,128)(2,1)S(1)}, u32[]{:S(2)}, u32[]{:S(2)}) collective-permute-start(bf16[1024,128]{1,0:T(8,128)(2,1)S(1)} %get-tuple-element.27), channel_id=1, source_target_pairs={{0,384},{32,416},{64,448},{96,480},{128,0},{160,32},{192,64},{224,... | collective-permute-start | bytes 786440 | tf_op jit(solution)/shard_map/scatter_q_relay/ppermute | solution.py:45
  123.9 20.4 %collective-permute-start.15 = (bf16[16,2,128,128]{3,2,1,0:T(8,128)(2,1)S(1)}, bf16[16,2,128,128]{3,2,1,0:T(8,128)(2,1)S(1)}, u32[]{:S(2)}, u32[]{:S(2)}) collective-permute-start(bf16[16,2,128,128]{3,2,1,0:T(8,128)(2,1)S(1)} %copy-done.5), channel_id=1, source_target_pairs={{0,1},{1,0},{2,3},{3,2},{4,5},{5,4},{6,7},{7,6},{8,9},{9,8},{10,11... | collective-permute-start | bytes 3145736 | tf_op jit(solution)/shard_map/scatter_kv_core/ppermute | solution.py:53
  125.8 14.7 %collective-permute-start.9 = (bf16[1024,128]{1,0:T(8,128)(2,1)S(1)}, bf16[1024,128]{1,0:T(8,128)(2,1)S(1)}, u32[]{:S(2)}, u32[]{:S(2)}) collective-permute-start(bf16[1024,128]{1,0:T(8,128)(2,1)S(1)} %get-tuple-element.26), channel_id=1, source_target_pairs={{0,128},{32,160},{64,192},{96,224},{128,256},{160,288},{192,320},{... | collective-permute-start | bytes 786440 | tf_op jit(solution)/shard_map/scatter_q_relay/ppermute | solution.py:45
  134.0 10.2 %copy-start = (bf16[16,2,128,128]{3,2,1,0:T(8,128)(2,1)S(1)}, bf16[16,2,128,128]{3,2,1,0:T(8,128)(2,1)}, u32[]{:S(2)}) copy-start(bf16[16,2,128,128]{3,2,1,0:T(8,128)(2,1)} %get-tuple-element.19) | copy-start | bytes 3145732
  134.1 18.8 %collective-permute-start.12 = (bf16[2048,128]{1,0:T(8,128)(2,1)S(1)}, bf16[2048,128]{1,0:T(8,128)(2,1)S(1)}, u32[]{:S(2)}, u32[]{:S(2)}) collective-permute-start(bf16[2048,128]{1,0:T(8,128)(2,1)S(1)} %add_convert_fusion.2), channel_id=1, source_target_pairs={{0,384},{32,416},{64,448},{96,480},{128,0},{160,32},{192,64},{224,... | collective-permute-start | bytes 1572872 | tf_op jit(solution)/shard_map/scatter_q_x/ppermute | solution.py:45
  140.6 16.8 %collective-permute-start.10 = (bf16[2048,128]{1,0:T(8,128)(2,1)S(1)}, bf16[2048,128]{1,0:T(8,128)(2,1)}, u32[]{:S(2)}, u32[]{:S(2)}) collective-permute-start(bf16[2048,128]{1,0:T(8,128)(2,1)S(1)} %add_convert_fusion.3), channel_id=1, source_target_pairs={{0,128},{32,160},{64,192},{96,224},{128,256},{160,288},{192,320},{... | collective-permute-start | bytes 1572872 | tf_op jit(solution)/shard_map/scatter_q_x/ppermute | solution.py:45
  145.6 22.8 %all-to-all-start.2 = ((bf16[4,4,2,128,128]{4,3,2,1,0:T(8,128)(2,1)}), bf16[4,4,2,128,128]{4,3,2,1,0:T(8,128)(2,1)S(1)}, u32[]{:S(2)}, u32[]{:S(2)}) async-start(bf16[4,4,2,128,128]{4,3,2,1,0:T(8,128)(2,1)} %bitcast.34), calls=%async_computation.2 | async-start | bytes 2097152 | tf_op jit(solution)/shard_map/scatter_kv_y/all_to_all | solution.py:36
  158.7 26.9 %collective-permute-start.13 = (bf16[2,512,128]{2,1,0:T(8,128)(2,1)S(1)}, bf16[2,512,128]{2,1,0:T(8,128)(2,1)S(1)}, u32[]{:S(2)}, u32[]{:S(2)}) collective-permute-start(bf16[2,512,128]{2,1,0:T(8,128)(2,1)S(1)} %slice.51), channel_id=1, source_target_pairs={{0,32},{32,0},{64,96},{96,64},{128,160},{160,128},{192,224},{224,1... | collective-permute-start | bytes 786440 | tf_op jit(solution)/shard_map/scatter_q_zl/ppermute | solution.py:49
  169.3 36.1 %all-to-all-start.3 = ((bf16[4,2,128,128]{3,2,1,0:T(8,128)(2,1)}), bf16[4,2,128,128]{3,2,1,0:T(8,128)(2,1)S(1)}, u32[]{:S(2)}, u32[]{:S(2)}) async-start(bf16[4,2,128,128]{3,2,1,0:T(8,128)(2,1)} %fusion), calls=%async_computation.3 | async-start | bytes 524288 | tf_op jit(solution)/shard_map/scatter_kv_deal/all_to_all | solution.py:36
  185.6 15.3 %collective-permute-start.14 = (bf16[512,128]{1,0:T(8,128)(2,1)S(1)}, bf16[512,128]{1,0:T(8,128)(2,1)S(1)}, u32[]{:S(2)}, u32[]{:S(2)}) collective-permute-start(bf16[512,128]{1,0:T(8,128)(2,1)S(1)} %slice_bitcast_fusion), channel_id=1, source_target_pairs={{0,64},{32,96},{64,0},{96,32},{128,192},{160,224},{192,128},{224,1... | collective-permute-start | bytes 393224 | tf_op jit(solution)/shard_map/scatter_q_zl/ppermute | solution.py:49

commit v2 on v1

--- a/solution.py
+++ b/solution.py
@@ -11,7 +11,7 @@
 NX, NZL, NY, NZH, NCORE = 4, 4, 4, 4, 2
 SEGMENTS = 11
 LOG2E = 1.4426950408889634
-ROUND = 4
+ROUNDS = (4, 2, 1)
 
 
 def flat(x, zl, y, zh, core):
@@ -47,6 +47,15 @@
 
 def flip_zl(value, bits):
     return lax.ppermute(value, "row", [(row, row ^ bits) for row in range(NX * NZL)])
+
+
+def flip_deal(value, bits):
+    pairs = []
+    for x, zl, y, zh, core in spans(NX, NZL, NY, NZH, NCORE):
+        back = (zh ^ bits) - zh
+        there = flat((x - back) % NX, (zl - back) % NZL, y, zh ^ bits, core)
+        pairs.append((flat(x, zl, y, zh, core), there))
+    return lax.ppermute(value, ("row", "col"), pairs)
 
 
 def flip_core(value):
@@ -72,13 +81,65 @@
     return jnp.stack([start, low, high, finish])
 
 
-def attention_kernel(jcount, ids_ref, table_ref, *refs):
+def list_kernel(jcount, ids_ref, table_ref, items_ref, count_ref):
+    my_c, deal_x, deal_zl = ids_ref[2], ids_ref[3], ids_ref[4]
+    firsts = []
+    for slot in range(16):
+        group = ((deal_x - slot) & 3) * 4 + ((deal_zl - slot) & 3)
+        firsts.append((group * 16 + slot) * 256)
+
+    def list_block(j, counts):
+        base = (j * 32 + my_c) * 128
+        first_low, last_low = jnp.int32(0), jnp.int32(0)
+        hull_low, hull_high = jnp.int32(1 << 30), jnp.int32(0)
+        for s in range(SEGMENTS):
+            start, low, high = table_ref[0, s], table_ref[1, s], table_ref[2, s]
+            finish = table_ref[3, s]
+            first_low = jnp.where(base >= start, start, first_low)
+            last_low = jnp.where(base + 127 >= start, start, last_low)
+            meets = (start <= base + 127) & (finish > base) & (finish > start)
+            hull_low = jnp.where(meets, jnp.minimum(hull_low, low), hull_low)
+            hull_high = jnp.where(meets, jnp.maximum(hull_high, high), hull_high)
+        hull_high = jnp.minimum(hull_high, base + 128)
+        single = first_low == last_low
+        tile_high = jnp.where(single, jnp.minimum(hull_high, base + 1), 0)
+        fulls, parts = counts
+        for slot, first in enumerate(firsts):
+            own = (first <= base + 127) & (first + 255 >= first_low)
+            active = own | ((first < hull_high) & (first + 255 >= hull_low))
+            full = (first >= last_low) & (first + 255 <= base)
+            full = full | ((first >= hull_low) & (first + 256 <= tile_high))
+            items_ref[0, fulls] = j * 16 + slot
+            items_ref[1, parts] = j * 16 + slot
+            fulls = fulls + jnp.where(active & full, 1, 0)
+            parts = parts + jnp.where(active & jnp.logical_not(full), 1, 0)
+        return fulls, parts
+
+    zero = jnp.int32(0)
+    count_ref[0], count_ref[1] = lax.fori_loop(0, jcount, list_block, (zero, zero))
+
+
+def list_items(ids, table, jcount):
+    smem = pl.BlockSpec(memory_space=pltpu.SMEM)
+    return pl.pallas_call(
+        functools.partial(list_kernel, jcount),
+        out_shape=[
+            jax.ShapeDtypeStruct((2, jcount * 16 + 1), jnp.int32),
+            jax.ShapeDtypeStruct((2,), jnp.int32),
+        ],
+        in_specs=[smem] * 2,
+        out_specs=[smem] * 2,
+        name="list_items",
+    )(ids, table)
+
+
+def attention_kernel(jcount, ids_ref, table_ref, items_ref, count_ref, *refs):
     f32, bf16 = jnp.float32, jnp.bfloat16
     rows = jcount * 32
     own_ref, second_ref, outer_ref = refs[0:3]
     ahead_near, ahead_far, behind_near, behind_far, opposite_even, opposite_odd = refs[3:9]
-    kv0, kv1 = refs[9:11]
-    dqs, mine_ref, other_ref = refs[11:15], refs[15], refs[16]
+    kv0, kv1, mine_ref, other_ref = refs[9:11] + refs[15:17]
+    dqs = refs[11:15]
     (
         k_scr,
         v_scr,
@@ -96,12 +157,10 @@
         pre_low_scr,
         pre_high_scr,
         place_scr,
-        full_list,
-        part_list,
     ) = refs[17:]
     scale = 128.0 ** -0.5
     my_x, my_zl, my_c = ids_ref[0], ids_ref[1], ids_ref[2]
-    deal_x, deal_zl, my_core = ids_ref[3], ids_ref[4], ids_ref[5]
+    deal_x, deal_zl, my_core, my_zh = ids_ref[3], ids_ref[4], ids_ref[5], ids_ref[6]
 
     def source(xs, zs):
         if xs == 2:
@@ -128,15 +187,16 @@
     lane_part = lax.broadcasted_iota(jnp.int32, (4, 128), 1) >> 5
     for xs in range(NX):
         lanes = pl.ds(xs * 128, 128)
+        pieces = []
+        for zs in range(NZL):
+            aux = source(xs, zs)[pl.ds(2 * rows, 32), :].astype(f32)
+            pieces.append((aux[0:4] + aux[4:8] + aux[8:12], aux[12:16] + aux[16:20] + aux[20:24]))
         for b in range(4):
             lse = jnp.zeros((4, 128), f32)
             delta = jnp.zeros((4, 128), f32)
-            for zs in range(NZL):
-                aux = source(xs, zs)[pl.ds(2 * rows, 32), :].astype(f32)
+            for zs, (lse_part, delta_part) in enumerate(pieces):
                 turn = ((zs - b) * 32) % 128
                 here = lane_part == zs
-                lse_part = aux[0:4] + aux[4:8] + aux[8:12]
-                delta_part = aux[12:16] + aux[16:20] + aux[20:24]
                 if turn:
                     lse_part = pltpu.roll(lse_part, turn, 1)
                     delta_part = pltpu.roll(delta_part, turn, 1)
@@ -169,40 +229,7 @@
     def first_of(slot):
         return (group_of(slot & 3) * 16 + slot) * 256
 
-    def sort_block(j, counts):
-        base = (j * 32 + my_c) * 128
-        first_low, last_low = jnp.int32(0), jnp.int32(0)
-        hull_low, hull_high = jnp.int32(1 << 30), jnp.int32(0)
-        for s in range(SEGMENTS):
-            start, low, high = table_ref[0, s], table_ref[1, s], table_ref[2, s]
-            finish = table_ref[3, s]
-            first_low = jnp.where(base >= start, start, first_low)
-            last_low = jnp.where(base + 127 >= start, start, last_low)
-            meets = (start <= base + 127) & (finish > base) & (finish > start)
-            hull_low = jnp.where(meets, jnp.minimum(hull_low, low), hull_low)
-            hull_high = jnp.where(meets, jnp.maximum(hull_high, high), hull_high)
-        hull_high = jnp.minimum(hull_high, base + 128)
-        single = first_low == last_low
-        tile_high = jnp.where(single, jnp.minimum(hull_high, base + 1), 0)
-
-        def seek(zh, counts):
-            def look(y, counts):
-                fulls, parts = counts
-                slot = y * 4 + zh
-                first = first_of(slot)
-                active = (first <= base + 127) & (first + 255 >= first_low)
-                active = active | ((first < hull_high) & (first + 255 >= hull_low))
-                full = (first >= last_low) & (first + 255 <= base)
-                full = full | (single & (first >= hull_low) & (first + 256 <= tile_high))
-                full_list[fulls] = j * 16 + slot
-                part_list[parts] = j * 16 + slot
-                return (
-                    fulls + jnp.where(active & full, 1, 0),
-                    parts + jnp.where(active & jnp.logical_not(full), 1, 0),
-                )
-
-            return lax.fori_loop(0, jnp.where(group_of(zh) <= j, 4, 0), look, counts)
-
+    def take_block(j, _):
         for xs in range(NX):
             for zs in range(NZL):
                 at = (xs * NZL + zs) * 32
@@ -211,10 +238,9 @@
                 do_scr[j, pl.ds(at, 32), :] = ref[pl.ds(rows + j * 32, 32), :]
         qt_scr[j] = q_scr[j].T
         dot_scr[j] = do_scr[j].T
-        return lax.fori_loop(0, 4, seek, counts)
-
-    zero = jnp.int32(0)
-    full_count, part_count = lax.fori_loop(0, jcount, sort_block, (zero, zero))
+        return 0
+
+    lax.fori_loop(0, jcount, take_block, 0)
 
     def work(items, masked):
         items = [(item >> 4, item & 15) for item in items]
@@ -243,20 +269,21 @@
             dk_scr[slot] += jnp.dot(score_grad, q_scr[j], preferred_element_type=f32)
             dqt_scr[j] += jnp.dot(kt_scr[slot], score_grad, preferred_element_type=f32)
 
-    def sweep(items, count, masked):
-        begin = zero
-        for size in (ROUND, 1):
+    def sweep(kind, masked):
+        count = count_ref[kind]
+        begin = jnp.int32(0)
+        for size in ROUNDS:
             turns = (count - begin) // size
 
             def turn(at, _, begin=begin, size=size):
-                work([items[begin + at * size + u] for u in range(size)], masked)
+                work([items_ref[kind, begin + at * size + u] for u in range(size)], masked)
                 return 0
 
             lax.fori_loop(0, turns, turn, 0)
             begin = begin + turns * size
 
-    sweep(full_list, full_count, False)
-    sweep(part_list, part_count, True)
+    sweep(0, False)
+    sweep(1, True)
 
     def write_queries(j, _):
         dq = (dqt_scr[j] * scale).astype(bf16).T
@@ -269,25 +296,27 @@
     lax.fori_loop(0, jcount, write_queries, 0)
 
     def finish(slot, _):
+        bits = (slot & 3) ^ my_zh
+        out = (slot & 12) + jnp.where(bits == 3, 1, jnp.where(bits == 0, 0, bits + 1))
         for half, ref in enumerate((mine_ref, other_ref)):
             at = pl.ds(pl.multiple_of((half ^ my_core) * 128, 128), 128)
-            ref[slot, 0] = (dk_scr[slot, at, :] * scale).astype(bf16)
-            ref[slot, 1] = dv_scr[slot, at, :].astype(bf16)
+            ref[out, 0] = (dk_scr[slot, at, :] * scale).astype(bf16)
+            ref[out, 1] = dv_scr[slot, at, :].astype(bf16)
         return 0
 
     lax.fori_loop(0, 16, finish, 0)
 
 
-def run_attention(ids, table, payloads, kv0, kv1, jcount):
+def run_attention(ids, table, items, counts, payloads, kv0, kv1, jcount):
     f32, bf16 = jnp.float32, jnp.bfloat16
     rows = jcount * 32
     smem = pl.BlockSpec(memory_space=pltpu.SMEM)
     vmem = pl.BlockSpec(memory_space=pltpu.VMEM)
-    part = jax.ShapeDtypeStruct((NZL * rows, 128), bf16)
     return pl.pallas_call(
         functools.partial(attention_kernel, jcount),
-        out_shape=[part] * 4 + [jax.ShapeDtypeStruct((16, 2, 128, 128), bf16)] * 2,
-        in_specs=[smem] * 2 + [vmem] * 11,
+        out_shape=[jax.ShapeDtypeStruct((NZL * rows, 128), bf16)] * 4
+        + [jax.ShapeDtypeStruct((16, 2, 128, 128), bf16)] * 2,
+        in_specs=[smem] * 4 + [vmem] * 11,
         out_specs=[vmem] * 6,
         scratch_shapes=[
             pltpu.VMEM((16, 256, 128), bf16),
@@ -306,12 +335,10 @@
             pltpu.VMEM((jcount, 512), jnp.int32),
             pltpu.VMEM((jcount, 512), jnp.int32),
             pltpu.VMEM((jcount, 512), jnp.int32),
-            pltpu.SMEM((jcount * 16 + 1,), jnp.int32),
-            pltpu.SMEM((jcount * 16 + 1,), jnp.int32),
         ],
         compiler_params=pltpu.CompilerParams(vmem_limit_bytes=48 * 1024 * 1024),
         name="attention_backward",
-    )(ids, table, *payloads, kv0, kv1)
+    )(ids, table, items, counts, *payloads, kv0, kv1)
 
 
 def total(parts):
@@ -338,7 +365,7 @@
     row = lax.axis_index("row")
     col = lax.axis_index("col")
     my_x, my_zl, my_zh = row // NZL, row % NZL, (col // NCORE) % NZH
-    ids = jnp.stack([my_x, my_zl, col, my_x + my_zh, my_zl + my_zh, col % NCORE])
+    ids = jnp.stack([my_x, my_zl, col, my_x + my_zh, my_zl + my_zh, col % NCORE, my_zh])
     ids = ids.astype(jnp.int32)
 
     def heads_first(value):
@@ -372,12 +399,17 @@
         outer = flip_zl(jnp.stack([payload, second]), 1)
         others = jnp.concatenate([second[None], outer], axis=0)
     with jax.named_scope("gather_q_near"):
+        payload, second = lax.optimization_barrier((payload, second))
         near = [shift_x(payload, -1), shift_x(payload, 1)]
     with jax.named_scope("gather_kv_deal"):
         kv = gather(pair, DEALS)
     with jax.named_scope("gather_q_far"):
         others, *near = lax.optimization_barrier((others, *near))
         far = [shift_x(others, -1), shift_x(others, 1)]
+    with jax.named_scope("list_items"):
+        table = segment_table(segment, prefix)
+        items, counts = list_items(ids, table, jcount)
+        kv, items, counts = lax.optimization_barrier((kv, items, counts))
     with jax.named_scope("gather_kv_y"):
         kv = gather(kv, COLUMNS).reshape(NY * NZH, 2, 128, 128)
     with jax.named_scope("gather_q_relay"):
@@ -386,9 +418,8 @@
     with jax.named_scope("gather_kv_core"):
         kv_other = flip_core(kv)
 
-    table = segment_table(segment, prefix)
     payloads = [payload, second, outer, near[0], far[0], near[1], far[1], even, odd]
-    *dqs, mine, other = run_attention(ids, table, payloads, kv, kv_other, jcount)
+    *dqs, mine, other = run_attention(ids, table, items, counts, payloads, kv, kv_other, jcount)
 
     with jax.named_scope("scatter_kv_core"):
         mine = total([mine, flip_core(other)]).reshape(NY, NZH, 2, 128, 128)
@@ -402,7 +433,8 @@
         behind = total([dqs[3], jnp.concatenate([jnp.zeros_like(odd), odd])])
         dq = total([dqs[0], shift_x(ahead, 1), shift_x(behind, -1)])
     with jax.named_scope("scatter_kv_deal"):
-        mine = total(exchange(mine, DEALS))
+        mine = total([mine[:2], flip_deal(mine[2:], 1)])
+        mine = total([mine[0], flip_deal(mine[1], 3)])
     with jax.named_scope("scatter_q_zl"):
         dq = dq.reshape(NZL, rows, 128)
         dq = total([dq[0::2], flip_zl(dq[1::2], 1)])

time: 203 us -> 199 us (0.980)
  the two profiles are of different devices: /device:TPU:2 before, /device:TPU:400 now
where the time goes in v2:
time: 199 us; the launch traced here: 198 us
  starting transfers between devices  80.8 us (41%)
  waiting for transfers between devices  62.9 us (32%)
  Pallas kernels  35.2 us (18%)
  other arithmetic  12.3 us (6%)
  local copies, waits for them, and re-layouts  5.76 us (3%)
    ppermute x10, starting transfers between devices, shift_x(): return lax.ppermute(value, 'row', pairs)  40.2 us
    pallas_call x1, Pallas kernels, run_attention(): pl.pallas_call(functools.partial(attention_kernel, jcount), out_shape=[ja...  29.7 us
    ppermute x10, waiting for transfers between devices, shift_x(): return lax.ppermute(value, 'row', pairs)  26.8 us
    all_to_all x3, starting transfers between devices, exchange(): lax.all_to_all(value, ('row', 'col'), 0, 0, axis_index_groups=members)  23.6 us
    ppermute x2, waiting for transfers between devices, flip_deal(): return lax.ppermute(value, ('row', 'col'), pairs)  19.1 us
    ppermute x4, waiting for transfers between devices, flip_zl(): lax.ppermute(value, 'row', [(row, row ^ bits) for row in range(NX * NZL)])  13.9 us
    ppermute x4, starting transfers between devices, flip_zl(): lax.ppermute(value, 'row', [(row, row ^ bits) for row in range(NX * NZL)])  9.27 us
    pallas_call x1, Pallas kernels, list_items(): pl.pallas_call(functools.partial(list_kernel, jcount), out_shape=[jax.Sha...  5.51 us
  transfers between devices with their start and end apart: 21, of which 10 were waited for; matrix products, arithmetic and copies ran while one was open for 6% of the time, Pallas kernels for 3%

profile of v2, /device:TPU:400, one launch (start us, length us, event | category | flops | bytes accessed | tf_op | source)
XLA Modules:
  0.0 198.1 jit_solution(5986452099313441488)
XLA Ops:
  0.7 1.1 bitcast_reduce_fusion
  1.8 0.1 copy.17
  1.9 0.7 constant_dynamic-update-slice_fusion.5
  2.6 0.7 constant_dynamic-update-slice_fusion.4
  3.3 0.7 constant_dynamic-update-slice_fusion.3
  4.1 0.1 copy.18
  4.2 0.1 reshape.165
  4.3 0.1 pad.11.clone
  4.4 1.2 maximum_maximum_fusion.refs_0_
  5.5 0.0 copy-start.6
  5.5 0.0 copy-start.7
  5.6 3.5 %collective-permute-start = (bf16[1056,128]{1,0:T(8,128)(2,1)S(1)}, bf16[1056,128]{1,0:T(8,128)(2,1)S(1)}, u32[]{:S(2)}, u32[]{:S(2)}) collective-permute-start(bf16[1056,128]{1,0:T(8,128)(2,1)S(1)} %maximum_maximum_fusion.refs_0_), channel_id=1, source_target_pairs={{0,64},{32,96},{64,0},{96,32},{128,192},{160,224},{192,128},{224,1... | collective-permute-start | bytes 811016 | tf_op jit(solution)/shard_map/gather_q_zl/ppermute | solution.py:49
  9.1 0.7 broadcast_in_dim.59
  9.8 13.7 %all-to-all-start = ((bf16[4,2,128,128]{3,2,1,0:T(8,128)(2,1)}), bf16[4,2,128,128]{3,2,1,0:T(8,128)(2,1)S(1)}, u32[]{:S(2)}, u32[]{:S(2)}) async-start(bf16[4,2,128,128]{3,2,1,0:T(8,128)(2,1)} %broadcast_in_dim.59), calls=%async_computation | async-start | bytes 524288 | tf_op jit(solution)/shard_map/gather_kv_deal/all_to_all | solution.py:36
  23.5 0.1 pad_maximum_fusion.1
  23.6 1.9 collective-permute-start.1
  25.5 2.2 %convert_reduce_fusion.1 = (s32[11]{0:T(128)S(1)}, s32[11]{0:T(128)S(1)}, s32[11]{0:T(128)S(1)}) fusion(s32[65536]{0:T(1024)S(1)} %copy-done.6, s32[65536]{0:T(1024)S(1)} %copy-done.7), kind=kLoop, calls=%fused_computation.4 | loop fusion | flops 6488031 | bytes 524420 | tf_op jit(solution)/shard_map/list_items/reduce_sum | solution.py:75
  27.7 0.2 select_reduce_fusion.2
  27.9 6.2 %collective-permute-start.3 = (bf16[1056,128]{1,0:T(8,128)(2,1)S(1)}, bf16[1056,128]{1,0:T(8,128)(2,1)S(1)}, u32[]{:S(2)}, u32[]{:S(2)}) collective-permute-start(bf16[1056,128]{1,0:T(8,128)(2,1)S(1)} %maximum_maximum_fusion.refs_0_), channel_id=1, source_target_pairs={{0,128},{32,160},{64,192},{96,224},{128,256},{160,288},{192,320},{... | collective-permute-start | bytes 811016 | tf_op jit(solution)/shard_map/gather_q_near/ppermute | solution.py:45
  34.1 7.0 %collective-permute-start.2 = (bf16[1056,128]{1,0:T(8,128)(2,1)S(1)}, bf16[1056,128]{1,0:T(8,128)(2,1)S(1)}, u32[]{:S(2)}, u32[]{:S(2)}) collective-permute-start(bf16[1056,128]{1,0:T(8,128)(2,1)S(1)} %maximum_maximum_fusion.refs_0_), channel_id=1, source_target_pairs={{0,384},{32,416},{64,448},{96,480},{128,0},{160,32},{192,64},{224,... | collective-permute-start | bytes 811016 | tf_op jit(solution)/shard_map/gather_q_near/ppermute | solution.py:45
  41.1 0.6 pad_add_fusion.table_ref
  41.7 0.7 stack.77.ids_ref
  42.3 5.5 %list_items.1 = (s32[2,257]{1,0:T(2,128)}, s32[2]{0:T(128)}) custom-call(s32[7]{0:T(128)} %stack.77.ids_ref, s32[4,11]{1,0:T(4,128)} %pad_add_fusion.table_ref), custom_call_target="tpu_custom_call" | custom-call | tf_op jit(solution)/shard_map/list_items/list_items/pallas_call | solution.py:124
  47.9 1.2 broadcast_in_dim.61
  49.1 4.8 %all-to-all-start.1 = ((bf16[4,4,2,128,128]{4,3,2,1,0:T(8,128)(2,1)}), bf16[4,4,2,128,128]{4,3,2,1,0:T(8,128)(2,1)}, u32[]{:S(2)}, u32[]{:S(2)}) async-start(bf16[4,4,2,128,128]{4,3,2,1,0:T(8,128)(2,1)} %broadcast_in_dim.61), calls=%async_computation.1 | async-start | bytes 2097152 | tf_op jit(solution)/shard_map/gather_kv_y/all_to_all | solution.py:36
  53.9 1.0 pad_maximum_fusion
  54.9 2.1 %collective-permute-start.5 = (bf16[3,1056,128]{2,1,0:T(8,128)(2,1)}, bf16[3,1056,128]{2,1,0:T(8,128)(2,1)}, u32[]{:S(2)}, u32[]{:S(2)}) collective-permute-start(bf16[3,1056,128]{2,1,0:T(8,128)(2,1)} %pad_maximum_fusion), channel_id=1, source_target_pairs={{0,128},{32,160},{64,192},{96,224},{128,256},{160,288},{192,320},{... | collective-permute-start | bytes 2433032 | tf_op jit(solution)/shard_map/gather_q_far/ppermute | solution.py:45
  57.0 4.9 %collective-permute-start.4 = (bf16[3,1056,128]{2,1,0:T(8,128)(2,1)}, bf16[3,1056,128]{2,1,0:T(8,128)(2,1)S(1)}, u32[]{:S(2)}, u32[]{:S(2)}) collective-permute-start(bf16[3,1056,128]{2,1,0:T(8,128)(2,1)} %pad_maximum_fusion), channel_id=1, source_target_pairs={{0,384},{32,416},{64,448},{96,480},{128,0},{160,32},{192,64},{224,... | collective-permute-start | bytes 2433032 | tf_op jit(solution)/shard_map/gather_q_far/ppermute | solution.py:45
  61.9 3.0 %all-to-all-done.1 = bf16[4,4,2,128,128]{4,3,2,1,0:T(8,128)(2,1)} async-done(((bf16[4,4,2,128,128]{4,3,2,1,0:T(8,128)(2,1)}), bf16[4,4,2,128,128]{4,3,2,1,0:T(8,128)(2,1)}, u32[]{:S(2)}, u32[]{:S(2)}) %all-to-all-start.1) | async-done | bytes 1048608 | tf_op jit(solution)/shard_map/gather_kv_y/all_to_all | solution.py:36
  64.9 1.9 collective-permute-start.8
  66.8 9.5 %collective-permute-done.5.refs_6_ = bf16[3,1056,128]{2,1,0:T(8,128)(2,1)} collective-permute-done((bf16[3,1056,128]{2,1,0:T(8,128)(2,1)}, bf16[3,1056,128]{2,1,0:T(8,128)(2,1)}, u32[]{:S(2)}, u32[]{:S(2)}) %collective-permute-start.5) | collective-permute-done | bytes 811040 | tf_op jit(solution)/shard_map/gather_q_far/ppermute | solution.py:45
  76.3 1.1 slice.73
  77.4 0.0 copy-start
  77.4 1.9 collective-permute-start.7
  79.4 0.1 pad_maximum_fusion.2
  79.5 5.1 %collective-permute-start.6 = (bf16[2,1056,128]{2,1,0:T(8,128)(2,1)S(1)}, bf16[2,1056,128]{2,1,0:T(8,128)(2,1)S(1)}, u32[]{:S(2)}, u32[]{:S(2)}) collective-permute-start(bf16[2,1056,128]{2,1,0:T(8,128)(2,1)S(1)} %pad_maximum_fusion.2), channel_id=1, source_target_pairs={{0,384},{32,416},{64,448},{96,480},{128,0},{160,32},{192,64},{224,... | collective-permute-start | bytes 1622024 | tf_op jit(solution)/shard_map/gather_q_relay/ppermute | solution.py:45
  84.6 7.3 %collective-permute-done.7.refs_8_ = bf16[2,1056,128]{2,1,0:T(8,128)(2,1)S(1)} collective-permute-done((bf16[2,1056,128]{2,1,0:T(8,128)(2,1)S(1)}, bf16[2,1056,128]{2,1,0:T(8,128)(2,1)S(1)}, u32[]{:S(2)}, u32[]{:S(2)}) %collective-permute-start.7) | collective-permute-done | bytes 540704 | tf_op jit(solution)/shard_map/gather_q_relay/ppermute | solution.py:45
  91.9 1.3 collective-permute-done.6.refs_7_
  93.2 1.0 copy-done.5
  94.1 29.7 %attention_backward.1 = (bf16[2048,128]{1,0:T(8,128)(2,1)S(1)}, bf16[2048,128]{1,0:T(8,128)(2,1)S(1)}, bf16[2048,128]{1,0:T(8,128)(2,1)S(1)}, bf16[2048,128]{1,0...) custom-call(s32[7]{0:T(128)S(1)} %copy-done.1, s32[4,11]{1,0:T(4,128)S(1)} %copy-done, ...), custom_call_target="tpu_custom_call" | custom-call | tf_op jit(solution)/shard_map/attention_backward/pallas_call | solution.py:315
  123.9 3.9 %collective-permute-start.11 = (bf16[1024,128]{1,0:T(8,128)(2,1)S(1)}, bf16[1024,128]{1,0:T(8,128)(2,1)S(1)}, u32[]{:S(2)}, u32[]{:S(2)}) collective-permute-start(bf16[1024,128]{1,0:T(8,128)(2,1)S(1)} %get-tuple-element.41), channel_id=1, source_target_pairs={{0,384},{32,416},{64,448},{96,480},{128,0},{160,32},{192,64},{224,... | collective-permute-start | bytes 786440 | tf_op jit(solution)/shard_map/scatter_q_relay/ppermute | solution.py:45
  127.7 2.1 %collective-permute-start.9 = (bf16[1024,128]{1,0:T(8,128)(2,1)S(1)}, bf16[1024,128]{1,0:T(8,128)(2,1)S(1)}, u32[]{:S(2)}, u32[]{:S(2)}) collective-permute-start(bf16[1024,128]{1,0:T(8,128)(2,1)S(1)} %get-tuple-element.40), channel_id=1, source_target_pairs={{0,128},{32,160},{64,192},{96,224},{128,256},{160,288},{192,320},{... | collective-permute-start | bytes 786440 | tf_op jit(solution)/shard_map/scatter_q_relay/ppermute | solution.py:45
  129.9 1.9 collective-permute-start.15
  131.8 0.5 collective-permute-done.11
  132.3 0.1 add_convert_fusion.2
  132.4 5.1 %collective-permute-start.12 = (bf16[2048,128]{1,0:T(8,128)(2,1)S(1)}, bf16[2048,128]{1,0:T(8,128)(2,1)S(1)}, u32[]{:S(2)}, u32[]{:S(2)}) collective-permute-start(bf16[2048,128]{1,0:T(8,128)(2,1)S(1)} %add_convert_fusion.2), channel_id=1, source_target_pairs={{0,384},{32,416},{64,448},{96,480},{128,0},{160,32},{192,64},{224,... | collective-permute-start | bytes 1572872 | tf_op jit(solution)/shard_map/scatter_q_x/ppermute | solution.py:45
  137.5 0.1 add_convert_fusion.3
  137.5 1.9 collective-permute-start.10
  139.5 1.4 add_convert_fusion
  140.9 5.2 %all-to-all-start.2 = ((bf16[4,4,2,128,128]{4,3,2,1,0:T(8,128)(2,1)}), bf16[4,4,2,128,128]{4,3,2,1,0:T(8,128)(2,1)S(1)}, u32[]{:S(2)}, u32[]{:S(2)}) async-start(bf16[4,4,2,128,128]{4,3,2,1,0:T(8,128)(2,1)} %bitcast.35), calls=%async_computation.2 | async-start | bytes 2097152 | tf_op jit(solution)/shard_map/scatter_kv_y/all_to_all | solution.py:36
  146.0 2.8 %collective-permute-done.12 = bf16[2048,128]{1,0:T(8,128)(2,1)S(1)} collective-permute-done((bf16[2048,128]{1,0:T(8,128)(2,1)S(1)}, bf16[2048,128]{1,0:T(8,128)(2,1)S(1)}, u32[]{:S(2)}, u32[]{:S(2)}) %collective-permute-start.12) | collective-permute-done | bytes 524320 | tf_op jit(solution)/shard_map/scatter_q_x/ppermute | solution.py:45
  148.8 5.5 %collective-permute-done.10 = bf16[2048,128]{1,0:T(8,128)(2,1)} collective-permute-done((bf16[2048,128]{1,0:T(8,128)(2,1)S(1)}, bf16[2048,128]{1,0:T(8,128)(2,1)}, u32[]{:S(2)}, u32[]{:S(2)}) %collective-permute-start.10) | collective-permute-done | bytes 524320 | tf_op jit(solution)/shard_map/scatter_q_x/ppermute | solution.py:45
  154.4 1.2 add_convert_fusion.1
  155.6 1.9 collective-permute-start.13
  157.6 13.9 %collective-permute-done.13 = bf16[2,512,128]{2,1,0:T(8,128)(2,1)S(1)} collective-permute-done((bf16[2,512,128]{2,1,0:T(8,128)(2,1)S(1)}, bf16[2,512,128]{2,1,0:T(8,128)(2,1)S(1)}, u32[]{:S(2)}, u32[]{:S(2)}) %collective-permute-start.13) | collective-permute-done | bytes 262176 | tf_op jit(solution)/shard_map/scatter_q_zl/ppermute | solution.py:49
  171.5 0.1 add_convert_fusion.5
  171.6 0.1 add_convert_fusion.4
  171.7 1.9 collective-permute-start.16
  173.7 1.9 collective-permute-start.14
  175.6 6.9 %collective-permute-done.16 = bf16[2,2,128,128]{3,2,1,0:T(8,128)(2,1)S(1)} collective-permute-done((bf16[2,2,128,128]{3,2,1,0:T(8,128)(2,1)S(1)}, bf16[2,2,128,128]{3,2,1,0:T(8,128)(2,1)S(1)}, u32[]{:S(2)}, u32[]{:S(2)}) %collective-permute-start.16) | collective-permute-done | bytes 131104 | tf_op jit(solution)/shard_map/scatter_kv_deal/ppermute | solution.py:58
  182.6 1.9 collective-permute-start.17
  184.5 0.7 fusion.1
  185.2 12.2 %collective-permute-done.17 = bf16[2,128,128]{2,1,0:T(8,128)(2,1)S(1)} collective-permute-done((bf16[2,128,128]{2,1,0:T(8,128)(2,1)S(1)}, bf16[2,128,128]{2,1,0:T(8,128)(2,1)S(1)}, u32[]{:S(2)}, u32[]{:S(2)}) %collective-permute-start.17) | collective-permute-done | bytes 65568 | tf_op jit(solution)/shard_map/scatter_kv_deal/ppermute | solution.py:58
  197.5 0.6 slice_bitcast_fusion.6
  (42 shorter events, 0.3 us)
Async XLA Ops:
  0.6 8.5 %copy-start.8 = (bf16[128,128]{1,0:T(8,128)(2,1)S(1)}, bf16[128,128]{1,0:T(8,128)(2,1)}, u32[]{:S(2)}) copy-start(bf16[128,128]{1,0:T(8,128)(2,1)} %param.14) | copy-start | bytes 98308
  0.6 8.5 %copy-start.9 = (bf16[128,128]{1,0:T(8,128)(2,1)S(1)}, bf16[128,128]{1,0:T(8,128)(2,1)}, u32[]{:S(2)}) copy-start(bf16[128,128]{1,0:T(8,128)(2,1)} %param.13) | copy-start | bytes 98308
  5.5 20.0 %copy-start.6 = (s32[65536]{0:T(1024)S(1)}, s32[65536]{0:T(1024)}, u32[]{:S(2)}) copy-start(s32[65536]{0:T(1024)} %param.16) | copy-start | bytes 786436
  5.5 20.0 %copy-start.7 = (s32[65536]{0:T(1024)S(1)}, s32[65536]{0:T(1024)}, u32[]{:S(2)}) copy-start(s32[65536]{0:T(1024)} %param.17) | copy-start | bytes 786436
  5.6 18.0 %collective-permute-start = (bf16[1056,128]{1,0:T(8,128)(2,1)S(1)}, bf16[1056,128]{1,0:T(8,128)(2,1)S(1)}, u32[]{:S(2)}, u32[]{:S(2)}) collective-permute-start(bf16[1056,128]{1,0:T(8,128)(2,1)S(1)} %maximum_maximum_fusion.refs_0_), channel_id=1, source_target_pairs={{0,64},{32,96},{64,0},{96,32},{128,192},{160,224},{192,128},{224,1... | collective-permute-start | bytes 811016 | tf_op jit(solution)/shard_map/gather_q_zl/ppermute | solution.py:49
  9.8 38.0 %all-to-all-start = ((bf16[4,2,128,128]{3,2,1,0:T(8,128)(2,1)}), bf16[4,2,128,128]{3,2,1,0:T(8,128)(2,1)S(1)}, u32[]{:S(2)}, u32[]{:S(2)}) async-start(bf16[4,2,128,128]{3,2,1,0:T(8,128)(2,1)} %broadcast_in_dim.59), calls=%async_computation | async-start | bytes 524288 | tf_op jit(solution)/shard_map/gather_kv_deal/all_to_all | solution.py:36
  23.6 30.3 %collective-permute-start.1 = (bf16[2,1056,128]{2,1,0:T(8,128)(2,1)S(1)}, bf16[2,1056,128]{2,1,0:T(8,128)(2,1)S(1)}, u32[]{:S(2)}, u32[]{:S(2)}) collective-permute-start(bf16[2,1056,128]{2,1,0:T(8,128)(2,1)S(1)} %pad_maximum_fusion.1), channel_id=1, source_target_pairs={{0,32},{32,0},{64,96},{96,64},{128,160},{160,128},{192,224},{224,1... | collective-permute-start | bytes 1622024 | tf_op jit(solution)/shard_map/gather_q_zl/ppermute | solution.py:49
  27.9 26.9 %collective-permute-start.3 = (bf16[1056,128]{1,0:T(8,128)(2,1)S(1)}, bf16[1056,128]{1,0:T(8,128)(2,1)S(1)}, u32[]{:S(2)}, u32[]{:S(2)}) collective-permute-start(bf16[1056,128]{1,0:T(8,128)(2,1)S(1)} %maximum_maximum_fusion.refs_0_), channel_id=1, source_target_pairs={{0,128},{32,160},{64,192},{96,224},{128,256},{160,288},{192,320},{... | collective-permute-start | bytes 811016 | tf_op jit(solution)/shard_map/gather_q_near/ppermute | solution.py:45
  34.1 20.8 %collective-permute-start.2 = (bf16[1056,128]{1,0:T(8,128)(2,1)S(1)}, bf16[1056,128]{1,0:T(8,128)(2,1)S(1)}, u32[]{:S(2)}, u32[]{:S(2)}) collective-permute-start(bf16[1056,128]{1,0:T(8,128)(2,1)S(1)} %maximum_maximum_fusion.refs_0_), channel_id=1, source_target_pairs={{0,384},{32,416},{64,448},{96,480},{128,0},{160,32},{192,64},{224,... | collective-permute-start | bytes 811016 | tf_op jit(solution)/shard_map/gather_q_near/ppermute | solution.py:45
  49.1 15.8 %all-to-all-start.1 = ((bf16[4,4,2,128,128]{4,3,2,1,0:T(8,128)(2,1)}), bf16[4,4,2,128,128]{4,3,2,1,0:T(8,128)(2,1)}, u32[]{:S(2)}, u32[]{:S(2)}) async-start(bf16[4,4,2,128,128]{4,3,2,1,0:T(8,128)(2,1)} %broadcast_in_dim.61), calls=%async_computation.1 | async-start | bytes 2097152 | tf_op jit(solution)/shard_map/gather_kv_y/all_to_all | solution.py:36
  54.9 21.5 %collective-permute-start.5 = (bf16[3,1056,128]{2,1,0:T(8,128)(2,1)}, bf16[3,1056,128]{2,1,0:T(8,128)(2,1)}, u32[]{:S(2)}, u32[]{:S(2)}) collective-permute-start(bf16[3,1056,128]{2,1,0:T(8,128)(2,1)} %pad_maximum_fusion), channel_id=1, source_target_pairs={{0,128},{32,160},{64,192},{96,224},{128,256},{160,288},{192,320},{... | collective-permute-start | bytes 2433032 | tf_op jit(solution)/shard_map/gather_q_far/ppermute | solution.py:45
  57.0 22.4 %collective-permute-start.4 = (bf16[3,1056,128]{2,1,0:T(8,128)(2,1)}, bf16[3,1056,128]{2,1,0:T(8,128)(2,1)S(1)}, u32[]{:S(2)}, u32[]{:S(2)}) collective-permute-start(bf16[3,1056,128]{2,1,0:T(8,128)(2,1)} %pad_maximum_fusion), channel_id=1, source_target_pairs={{0,384},{32,416},{64,448},{96,480},{128,0},{160,32},{192,64},{224,... | collective-permute-start | bytes 2433032 | tf_op jit(solution)/shard_map/gather_q_far/ppermute | solution.py:45
  64.9 28.2 %collective-permute-start.8 = (bf16[16,2,128,128]{3,2,1,0:T(8,128)(2,1)}, bf16[16,2,128,128]{3,2,1,0:T(8,128)(2,1)S(1)}, u32[]{:S(2)}, u32[]{:S(2)}) collective-permute-start(bf16[16,2,128,128]{3,2,1,0:T(8,128)(2,1)} %bitcast.28.refs_9_), channel_id=1, source_target_pairs={{0,1},{1,0},{2,3},{3,2},{4,5},{5,4},{6,7},{7,6},{8,9},{9,8},{10,11... | collective-permute-start | bytes 3145736 | tf_op jit(solution)/shard_map/gather_kv_core/ppermute | solution.py:62
  77.4 16.7 %copy-start = (s32[4,11]{1,0:T(4,128)S(1)}, s32[4,11]{1,0:T(4,128)}, u32[]{:S(2)}) copy-start(s32[4,11]{1,0:T(4,128)} %pad_add_fusion.table_ref) | copy-start | bytes 532
  77.4 16.7 %copy-start.1 = (s32[7]{0:T(128)S(1)}, s32[7]{0:T(128)}, u32[]{:S(2)}) copy-start(s32[7]{0:T(128)} %stack.77.ids_ref) | copy-start | bytes 88
  77.4 16.7 %copy-start.2 = (s32[2,257]{1,0:T(2,128)S(1)}, s32[2,257]{1,0:T(2,128)}, u32[]{:S(2)}) copy-start(s32[2,257]{1,0:T(2,128)} %get-tuple-element.21.items_ref) | copy-start | bytes 6172
  77.4 16.7 %copy-start.3 = (s32[2]{0:T(128)S(1)}, s32[2]{0:T(128)}, u32[]{:S(2)}) copy-start(s32[2]{0:T(128)} %get-tuple-element.22.count_ref) | copy-start | bytes 28
  77.4 14.4 %collective-permute-start.7 = (bf16[2,1056,128]{2,1,0:T(8,128)(2,1)S(1)}, bf16[2,1056,128]{2,1,0:T(8,128)(2,1)S(1)}, u32[]{:S(2)}, u32[]{:S(2)}) collective-permute-start(bf16[2,1056,128]{2,1,0:T(8,128)(2,1)S(1)} %slice.73), channel_id=1, source_target_pairs={{0,128},{32,160},{64,192},{96,224},{128,256},{160,288},{192,320},{... | collective-permute-start | bytes 1622024 | tf_op jit(solution)/shard_map/gather_q_relay/ppermute | solution.py:45
  79.5 13.7 %collective-permute-start.6 = (bf16[2,1056,128]{2,1,0:T(8,128)(2,1)S(1)}, bf16[2,1056,128]{2,1,0:T(8,128)(2,1)S(1)}, u32[]{:S(2)}, u32[]{:S(2)}) collective-permute-start(bf16[2,1056,128]{2,1,0:T(8,128)(2,1)S(1)} %pad_maximum_fusion.2), channel_id=1, source_target_pairs={{0,384},{32,416},{64,448},{96,480},{128,0},{160,32},{192,64},{224,... | collective-permute-start | bytes 1622024 | tf_op jit(solution)/shard_map/gather_q_relay/ppermute | solution.py:45
  93.2 1.0 copy-start.5
  123.8 6.0 %copy-start.10 = (bf16[16,2,128,128]{3,2,1,0:T(8,128)(2,1)S(1)}, bf16[16,2,128,128]{3,2,1,0:T(8,128)(2,1)}, u32[]{:S(2)}) copy-start(bf16[16,2,128,128]{3,2,1,0:T(8,128)(2,1)} %get-tuple-element.34) | copy-start | bytes 3145732
  123.9 8.4 %collective-permute-start.11 = (bf16[1024,128]{1,0:T(8,128)(2,1)S(1)}, bf16[1024,128]{1,0:T(8,128)(2,1)S(1)}, u32[]{:S(2)}, u32[]{:S(2)}) collective-permute-start(bf16[1024,128]{1,0:T(8,128)(2,1)S(1)} %get-tuple-element.41), channel_id=1, source_target_pairs={{0,384},{32,416},{64,448},{96,480},{128,0},{160,32},{192,64},{224,... | collective-permute-start | bytes 786440 | tf_op jit(solution)/shard_map/scatter_q_relay/ppermute | solution.py:45
  127.7 9.7 %collective-permute-start.9 = (bf16[1024,128]{1,0:T(8,128)(2,1)S(1)}, bf16[1024,128]{1,0:T(8,128)(2,1)S(1)}, u32[]{:S(2)}, u32[]{:S(2)}) collective-permute-start(bf16[1024,128]{1,0:T(8,128)(2,1)S(1)} %get-tuple-element.40), channel_id=1, source_target_pairs={{0,128},{32,160},{64,192},{96,224},{128,256},{160,288},{192,320},{... | collective-permute-start | bytes 786440 | tf_op jit(solution)/shard_map/scatter_q_relay/ppermute | solution.py:45
  129.9 9.6 %collective-permute-start.15 = (bf16[16,2,128,128]{3,2,1,0:T(8,128)(2,1)S(1)}, bf16[16,2,128,128]{3,2,1,0:T(8,128)(2,1)S(1)}, u32[]{:S(2)}, u32[]{:S(2)}) collective-permute-start(bf16[16,2,128,128]{3,2,1,0:T(8,128)(2,1)S(1)} %copy-done.10), channel_id=1, source_target_pairs={{0,1},{1,0},{2,3},{3,2},{4,5},{5,4},{6,7},{7,6},{8,9},{9,8},{10,11... | collective-permute-start | bytes 3145736 | tf_op jit(solution)/shard_map/scatter_kv_core/ppermute | solution.py:62
  132.3 7.2 %copy-start.4 = (bf16[16,2,128,128]{3,2,1,0:T(8,128)(2,1)S(1)}, bf16[16,2,128,128]{3,2,1,0:T(8,128)(2,1)}, u32[]{:S(2)}) copy-start(bf16[16,2,128,128]{3,2,1,0:T(8,128)(2,1)} %get-tuple-element.33) | copy-start | bytes 3145732
  132.4 16.5 %collective-permute-start.12 = (bf16[2048,128]{1,0:T(8,128)(2,1)S(1)}, bf16[2048,128]{1,0:T(8,128)(2,1)S(1)}, u32[]{:S(2)}, u32[]{:S(2)}) collective-permute-start(bf16[2048,128]{1,0:T(8,128)(2,1)S(1)} %add_convert_fusion.2), channel_id=1, source_target_pairs={{0,384},{32,416},{64,448},{96,480},{128,0},{160,32},{192,64},{224,... | collective-permute-start | bytes 1572872 | tf_op jit(solution)/shard_map/scatter_q_x/ppermute | solution.py:45
  137.5 16.8 %collective-permute-start.10 = (bf16[2048,128]{1,0:T(8,128)(2,1)S(1)}, bf16[2048,128]{1,0:T(8,128)(2,1)}, u32[]{:S(2)}, u32[]{:S(2)}) collective-permute-start(bf16[2048,128]{1,0:T(8,128)(2,1)S(1)} %add_convert_fusion.3), channel_id=1, source_target_pairs={{0,128},{32,160},{64,192},{96,224},{128,256},{160,288},{192,320},{... | collective-permute-start | bytes 1572872 | tf_op jit(solution)/shard_map/scatter_q_x/ppermute | solution.py:45
  140.9 30.7 %all-to-all-start.2 = ((bf16[4,4,2,128,128]{4,3,2,1,0:T(8,128)(2,1)}), bf16[4,4,2,128,128]{4,3,2,1,0:T(8,128)(2,1)S(1)}, u32[]{:S(2)}, u32[]{:S(2)}) async-start(bf16[4,4,2,128,128]{4,3,2,1,0:T(8,128)(2,1)} %bitcast.35), calls=%async_computation.2 | async-start | bytes 2097152 | tf_op jit(solution)/shard_map/scatter_kv_y/all_to_all | solution.py:36
  155.6 15.9 %collective-permute-start.13 = (bf16[2,512,128]{2,1,0:T(8,128)(2,1)S(1)}, bf16[2,512,128]{2,1,0:T(8,128)(2,1)S(1)}, u32[]{:S(2)}, u32[]{:S(2)}) collective-permute-start(bf16[2,512,128]{2,1,0:T(8,128)(2,1)S(1)} %slice.60), channel_id=1, source_target_pairs={{0,32},{32,0},{64,96},{96,64},{128,160},{160,128},{192,224},{224,1... | collective-permute-start | bytes 786440 | tf_op jit(solution)/shard_map/scatter_q_zl/ppermute | solution.py:49
  171.7 10.8 %collective-permute-start.16 = (bf16[2,2,128,128]{3,2,1,0:T(8,128)(2,1)S(1)}, bf16[2,2,128,128]{3,2,1,0:T(8,128)(2,1)S(1)}, u32[]{:S(2)}, u32[]{:S(2)}) collective-permute-start(bf16[2,2,128,128]{3,2,1,0:T(8,128)(2,1)S(1)} %slice_bitcast_fusion), channel_id=1, source_target_pairs={{0,482},{1,483},{2,160},{3,161},{4,486},{5,487},{6,164},{7,165},{8... | collective-permute-start | bytes 393224 | tf_op jit(solution)/shard_map/scatter_kv_deal/ppermute | solution.py:58
  173.7 10.8 %collective-permute-start.14 = (bf16[512,128]{1,0:T(8,128)(2,1)S(1)}, bf16[512,128]{1,0:T(8,128)(2,1)S(1)}, u32[]{:S(2)}, u32[]{:S(2)}) collective-permute-start(bf16[512,128]{1,0:T(8,128)(2,1)S(1)} %slice_bitcast_fusion.2), channel_id=1, source_target_pairs={{0,64},{32,96},{64,0},{96,32},{128,192},{160,224},{192,128},{224,1... | collective-permute-start | bytes 393224 | tf_op jit(solution)/shard_map/scatter_q_zl/ppermute | solution.py:49
  182.6 14.9 %collective-permute-start.17 = (bf16[2,128,128]{2,1,0:T(8,128)(2,1)S(1)}, bf16[2,128,128]{2,1,0:T(8,128)(2,1)S(1)}, u32[]{:S(2)}, u32[]{:S(2)}) collective-permute-start(bf16[2,128,128]{2,1,0:T(8,128)(2,1)S(1)} %slice_bitcast_fusion.4), channel_id=1, source_target_pairs={{0,166},{1,167},{2,484},{3,485},{4,162},{5,163},{6,480},{7,481},{8... | collective-permute-start | bytes 196616 | tf_op jit(solution)/shard_map/scatter_kv_deal/ppermute | solution.py:58
